TPU v7x, 32 devices: a whole 2x2x4 slice. The times are simulated.
32 devices in a mesh: dp: 8 (over y, x, core), tensor: 4 (over z).
Axes of the slice: x: 2, y: 2, z: 4, core: 2. Of those that a mesh axis runs over, the one named last changes fastest.
Arguments:
- inputs: bfloat16 [1, 16384, 768], P(None, ('dp', 'tensor')), may hold values from -6 to 6
- lengths: int32 [8, 1, 4], P('dp'), may hold values from 1 to 2045, as said below
- w_qkv: bfloat16 [3, 768, 768], P(None, 'dp', 'tensor'), may hold values from -0.21875 to 0.21875
- b_qv: bfloat16 [2, 768], P(None, 'tensor'), may hold values from -3 to 3
- w_out: bfloat16 [768, 768], P('tensor', 'dp'), may hold values from -0.875 to 0.875
- b_out: bfloat16 [768], replicated, may hold values from -3 to 3
- w_fc: bfloat16 [768, 3072], P('dp', 'tensor'), may hold values from -0.21875 to 0.21875
- b_fc: bfloat16 [3072], P('tensor'), may hold values from -3 to 3
- w_proj: bfloat16 [3072, 768], P('tensor', 'dp'), may hold values from -0.109375 to 0.109375
- b_proj: bfloat16 [768], replicated, may hold values from -3 to 3
- gain_one: bfloat16 [768], replicated, may hold values from 0.5 to 1.5
- shift_one: bfloat16 [768], replicated, may hold values from -2 to 2
- gain_two: bfloat16 [768], replicated, may hold values from 0.5 to 1.5
- shift_two: bfloat16 [768], replicated, may hold values from -2 to 2
- cotangent: bfloat16 [1, 16384, 768], P(None, ('dp', 'tensor')), may hold values from -6 to 6
Outputs:
- output: bfloat16 [1, 16384, 768], P(None, ('dp', 'tensor'))
- grad_inputs: float32 [1, 16384, 768], P(None, ('dp', 'tensor'))
- d_w_qkv: float32 [3, 768, 768], P(None, 'dp', 'tensor')
- d_b_qv: float32 [2, 768], P(None, 'tensor')
- d_w_out: float32 [768, 768], P('tensor', 'dp')
- d_b_out: float32 [768], replicated
- d_w_fc: float32 [768, 3072], P('dp', 'tensor')
- d_b_fc: float32 [3072], P('tensor')
- d_w_proj: float32 [3072, 768], P('tensor', 'dp')
- d_b_proj: float32 [768], replicated
- d_gain_one: float32 [768], replicated
- d_shift_one: float32 [768], replicated
- d_gain_two: float32 [768], replicated
- d_shift_two: float32 [768], replicated
Inputs may be any that keep to these rules, and one draw needn't show every extreme that they name: The 4 lengths of one pack sum to at most 2048.
All inputs are finite; a program needn't handle non-finite values.
Results may differ from a plain program's by a relative error of at most 0.0098.
Values may be sent and summed in bfloat16 or wider, within the bound.
No kernel may reach another device: no remote copies, remote signals or barrier semaphores. Data moves between devices by JAX's collectives and lax.ppermute only.
A program may use at most 192 MiB of HBM per device.

v0:
```python
from functools import partial

import jax
import jax.numpy as jnp
from jax import lax
from jax.sharding import PartitionSpec as P

HEAD_DIM = 64


EPSILON = 1e-05
MASKED = -1000000000.0


def in_blocks(shard, dim, devices):
    shape = shard.shape
    tiles = shard.reshape(*shape[:dim], devices, shape[dim] // devices, *shape[dim + 1 :])
    return jnp.moveaxis(tiles, dim, 0)


def sum_at_owner(shard, axis, dim):
    devices = lax.axis_size(axis)
    tiles = lax.all_to_all(in_blocks(shard, dim, devices), axis, 0, 0, tiled=True)
    return jnp.sum(tiles.astype(jnp.float32), axis=0)


def norm_parts(row_vals):
    row_mean = jnp.mean(row_vals, axis=-1, keepdims=True)
    centred = row_vals - row_mean
    inverse = lax.rsqrt(jnp.mean(centred * centred, axis=-1, keepdims=True) + EPSILON)
    return (centred * inverse, inverse)


def norm_back(grad_normed, normed, inverse):
    first_mean = jnp.mean(grad_normed, axis=-1, keepdims=True)
    second_mean = jnp.mean(grad_normed * normed, axis=-1, keepdims=True)
    return inverse * (grad_normed - first_mean - normed * second_mean)


def doc_ids(pack_lengths, pack_len):
    seq_count = pack_lengths.shape[0]
    seq_ends = jnp.cumsum(pack_lengths, dtype=jnp.int32)
    places = jnp.arange(pack_len, dtype=jnp.int32)
    passed = jnp.sum(
        (places[:, None] >= seq_ends[None, :]).astype(jnp.int32), axis=1, dtype=jnp.int32
    )
    return jnp.where(passed < seq_count, passed, seq_count + places)


def allowed_block(doc_of, first_row, block_rows):
    finish = first_row + block_rows
    query_pos = jnp.arange(first_row, finish)
    key_pos = jnp.arange(finish)
    causal = key_pos[None, :] <= query_pos[:, None]
    return causal & (doc_of[first_row:finish, None] == doc_of[None, :finish])


def block_scores(query_block, key_rows, doc_of, first_row, block_rows, scale):
    finish = first_row + block_rows
    scores = (
        jnp.einsum(
            "qhe,khe->hqk", query_block, key_rows[:finish], preferred_element_type=jnp.float32
        )
        * scale
    )
    return jnp.where(allowed_block(doc_of, first_row, block_rows)[None], scores, MASKED)


def attend_forward(queries, key_rows, values, doc_of, block_rows, scale):
    outputs, log_sums = ([], [])
    for first_row in range(0, queries.shape[0], block_rows):
        finish = first_row + block_rows
        scores = block_scores(
            queries[first_row:finish], key_rows, doc_of, first_row, block_rows, scale
        )
        row_max = jnp.max(scores, axis=-1, keepdims=True)
        exponent = jnp.exp(scores - row_max)
        row_total = jnp.sum(exponent, axis=-1, keepdims=True)
        attn_probs = (exponent / row_total).astype(jnp.bfloat16)
        outputs.append(
            jnp.einsum(
                "hqk,khe->qhe", attn_probs, values[:finish], preferred_element_type=jnp.float32
            )
        )
        log_sums.append(row_max + jnp.log(row_total))
    return (jnp.concatenate(outputs, axis=0), log_sums)


def attend_backward(queries, key_rows, values, grad_att, doc_of, log_sums, block_rows, scale):
    grad_queries = []
    grad_keys = jnp.zeros(key_rows.shape, jnp.float32)
    grad_values = jnp.zeros(values.shape, jnp.float32)
    for block_num, first_row in enumerate(range(0, queries.shape[0], block_rows)):
        finish = first_row + block_rows
        query_block = queries[first_row:finish]
        grad_block = grad_att[first_row:finish]
        scores = block_scores(query_block, key_rows, doc_of, first_row, block_rows, scale)
        attn_probs = jnp.exp(scores - log_sums[block_num])
        grad_probs = jnp.einsum(
            "qhe,khe->hqk", grad_block, values[:finish], preferred_element_type=jnp.float32
        )
        row_delta = jnp.sum(attn_probs * grad_probs, axis=-1, keepdims=True)
        grad_scores = (attn_probs * (grad_probs - row_delta)).astype(jnp.bfloat16)
        grad_queries.append(
            scale
            * jnp.einsum(
                "hqk,khe->qhe", grad_scores, key_rows[:finish], preferred_element_type=jnp.float32
            )
        )
        grad_keys = grad_keys.at[:finish].add(
            scale
            * jnp.einsum(
                "hqk,qhe->khe", grad_scores, query_block, preferred_element_type=jnp.float32
            )
        )
        grad_values = grad_values.at[:finish].add(
            jnp.einsum(
                "hqk,qhe->khe",
                attn_probs.astype(jnp.bfloat16),
                grad_block,
                preferred_element_type=jnp.float32,
            )
        )
    return (jnp.concatenate(grad_queries, axis=0), grad_keys, grad_values)


def rows_gather(rows_low):
    return lax.all_gather(rows_low, "tensor", axis=0, tiled=True)


def rows_sum(term_fn, row_count):
    return lax.psum_scatter(
        term_fn(jnp.int32(0), lax.axis_size("tensor") * row_count),
        "tensor",
        scatter_dimension=0,
        tiled=True,
    )


def grads_gather(rows_low):
    return lax.all_gather(rows_low, "tensor", axis=0, tiled=True)


def grads_sum(term_fn, row_count):
    return lax.psum_scatter(
        term_fn(jnp.int32(0), lax.axis_size("tensor") * row_count),
        "tensor",
        scatter_dimension=0,
        tiled=True,
    )


def on_device(
    inputs,
    lengths,
    w_qkv,
    b_qv,
    w_out,
    b_out,
    w_fc,
    b_fc,
    w_proj,
    b_proj,
    gain_one,
    shift_one,
    gain_two,
    shift_two,
    cotangent,
):
    pack_count, row_count, model_width = inputs.shape
    tensor_size = lax.axis_size("tensor")
    pack_len = row_count * tensor_size
    head_width = w_qkv.shape[2]
    local_heads = head_width // HEAD_DIM
    block_rows = min(512, pack_len)
    scale = HEAD_DIM ** (-0.5)
    fc_local = b_fc.shape[0]
    qkv_full, out_full = (
        lax.all_gather(w_qkv, "dp", axis=1, tiled=True),
        lax.all_gather(w_out, "dp", axis=1, tiled=True),
    )
    fc_full, proj_full = (
        lax.all_gather(w_fc, "dp", axis=0, tiled=True),
        lax.all_gather(w_proj, "dp", axis=1, tiled=True),
    )
    fc_bias = b_fc.astype(jnp.float32)
    bias_query = b_qv[0].astype(jnp.float32)
    bias_value = b_qv[1].astype(jnp.float32)
    bias_out = b_out.astype(jnp.float32)
    bias_proj = b_proj.astype(jnp.float32)
    gain_first = gain_one.astype(jnp.float32)
    shift_first = shift_one.astype(jnp.float32)
    gain_second = gain_two.astype(jnp.float32)
    shift_second = shift_two.astype(jnp.float32)
    grad_proj_w = jnp.zeros(proj_full.shape, jnp.float32)
    gelu_tanh = partial(jax.nn.gelu, approximate=True)
    outputs, grads_in = ([], [])
    doc_of = doc_ids(lengths[0, 0], pack_len)
    rows_in = inputs[0].astype(jnp.float32)
    normed_one, inverse_one = norm_parts(rows_in)
    h_one = (normed_one * gain_first + shift_first).astype(jnp.bfloat16)
    h_one_all = rows_gather(h_one)
    projected = jnp.einsum("td,sde->ste", h_one_all, qkv_full, preferred_element_type=jnp.float32)
    queries = (
        (projected[0] + bias_query).astype(jnp.bfloat16).reshape(pack_len, local_heads, HEAD_DIM)
    )
    key_rows = projected[1].astype(jnp.bfloat16).reshape(pack_len, local_heads, HEAD_DIM)
    values = (
        (projected[2] + bias_value).astype(jnp.bfloat16).reshape(pack_len, local_heads, HEAD_DIM)
    )
    attended, log_sums = attend_forward(queries, key_rows, values, doc_of, block_rows, scale)
    att_low = attended.reshape(pack_len, head_width).astype(jnp.bfloat16)

    def attn_term(first_row, row_span):
        return jnp.dot(att_low, out_full, preferred_element_type=jnp.float32)

    middle = rows_in + rows_sum(attn_term, row_count) + bias_out
    normed_two, inverse_two = norm_parts(middle)
    h_two = (normed_two * gain_second + shift_second).astype(jnp.bfloat16)
    h_two_all = rows_gather(h_two)
    pre_act = jnp.dot(h_two_all, fc_full, preferred_element_type=jnp.float32) + fc_bias
    active, gelu_back = jax.vjp(gelu_tanh, pre_act)
    active_low = active.astype(jnp.bfloat16)

    def mlp_term(first_row, row_span):
        return jnp.dot(
            lax.dynamic_slice_in_dim(active_low, first_row, row_span, 0),
            proj_full,
            preferred_element_type=jnp.float32,
        )

    mlp_out = rows_sum(mlp_term, row_count)
    outputs.append((middle + mlp_out + bias_proj).astype(jnp.bfloat16))
    grad_y = cotangent[0].astype(jnp.float32)
    acc_bias_proj = jnp.sum(grad_y, axis=0)
    grad_low = cotangent[0]
    grad_low_all = grads_gather(grad_low)
    grad_proj_w = grad_proj_w + jnp.einsum(
        "tf,td->fd", active_low, grad_low_all, preferred_element_type=jnp.float32
    )
    grad_active = jnp.einsum(
        "td,fd->tf", grad_low_all, proj_full, preferred_element_type=jnp.float32
    )
    grad_pre = gelu_back(grad_active)[0].astype(jnp.bfloat16)
    sum_bias_fc = jnp.sum(grad_pre, axis=0, dtype=jnp.float32)
    grad_fc_w = jnp.einsum("td,tf->df", h_two_all, grad_pre, preferred_element_type=jnp.float32)

    def fc_back_term(first_row, row_span):
        return jnp.einsum("tf,df->td", grad_pre, fc_full, preferred_element_type=jnp.float32)

    grad_h_two = grads_sum(fc_back_term, row_count)
    acc_gain_two = jnp.sum(grad_h_two * normed_two, axis=0)
    acc_shift_two = jnp.sum(grad_h_two, axis=0)
    grad_middle = grad_y + norm_back(grad_h_two * gain_second, normed_two, inverse_two)
    acc_bias_out = jnp.sum(grad_middle, axis=0)
    grad_mid_all = grads_gather(grad_middle.astype(jnp.bfloat16))
    grad_out_w = jnp.einsum("tc,td->cd", att_low, grad_mid_all, preferred_element_type=jnp.float32)
    grad_att = jnp.einsum(
        "td,cd->tc", grad_mid_all, out_full, preferred_element_type=jnp.float32
    ).astype(jnp.bfloat16)
    grad_att = grad_att.reshape(pack_len, local_heads, HEAD_DIM)
    grad_query, grad_key, grad_value = attend_backward(
        queries, key_rows, values, grad_att, doc_of, log_sums, block_rows, scale
    )
    stacked = jnp.stack(
        [
            grad_query.reshape(pack_len, head_width),
            grad_key.reshape(pack_len, head_width),
            grad_value.reshape(pack_len, head_width),
        ]
    ).astype(jnp.bfloat16)
    sum_qv = jnp.stack(
        [
            jnp.sum(stacked[0], axis=0, dtype=jnp.float32),
            jnp.sum(stacked[2], axis=0, dtype=jnp.float32),
        ]
    )
    grad_qkv_w = jnp.einsum("td,ste->sde", h_one_all, stacked, preferred_element_type=jnp.float32)

    def input_term(first_row, row_span):
        return jnp.einsum("ste,sde->td", stacked, qkv_full, preferred_element_type=jnp.float32)

    grad_h_one = grads_sum(input_term, row_count)
    acc_gain_one = jnp.sum(grad_h_one * normed_one, axis=0)
    acc_shift_one = jnp.sum(grad_h_one, axis=0)
    grads_in.append(grad_middle + norm_back(grad_h_one * gain_first, normed_one, inverse_one))
    grad_qkv_w, grad_out_w = (
        lax.psum_scatter(grad_qkv_w, "dp", scatter_dimension=1, tiled=True),
        lax.psum_scatter(grad_out_w, "dp", scatter_dimension=1, tiled=True),
    )
    grad_fc_w, grad_proj_w = (
        sum_at_owner(grad_fc_w.astype(jnp.bfloat16), "dp", 0),
        sum_at_owner(grad_proj_w.astype(jnp.bfloat16), "dp", 1),
    )
    tensor_pos = lax.axis_index("tensor")
    qv_placed = lax.dynamic_update_slice(
        jnp.zeros((2, model_width), jnp.float32), sum_qv, (0, tensor_pos * head_width)
    )
    fc_placed = lax.dynamic_update_slice(
        jnp.zeros((fc_local * tensor_size,), jnp.float32), sum_bias_fc, (tensor_pos * fc_local,)
    )
    packed = jnp.concatenate(
        [
            acc_gain_one,
            acc_shift_one,
            acc_gain_two,
            acc_shift_two,
            acc_bias_out,
            acc_bias_proj,
            qv_placed.reshape(-1),
            fc_placed,
        ]
    )
    summed = lax.psum(packed, ("dp", "tensor"))
    qv_total = summed[6 * model_width : 8 * model_width].reshape(2, model_width)
    grad_b_qv = lax.dynamic_slice(qv_total, (0, tensor_pos * head_width), (2, head_width))
    grad_b_fc = lax.dynamic_slice(summed[8 * model_width :], (tensor_pos * fc_local,), (fc_local,))
    return (
        jnp.stack(outputs),
        jnp.stack(grads_in),
        grad_qkv_w,
        grad_b_qv,
        grad_out_w,
        summed[4 * model_width : 5 * model_width],
        grad_fc_w,
        grad_b_fc,
        grad_proj_w,
        summed[5 * model_width : 6 * model_width],
        summed[0:model_width],
        summed[model_width : 2 * model_width],
        summed[2 * model_width : 3 * model_width],
        summed[3 * model_width : 4 * model_width],
    )


def solution(mesh):
    placed = (
        P(None, ("dp", "tensor"), None),
        P("dp", None, None),
        P(None, "dp", "tensor"),
        P(None, "tensor"),
        P("tensor", "dp"),
        P(),
        P("dp", "tensor"),
        P("tensor"),
        P("tensor", "dp"),
        P(),
        P(),
        P(),
        P(),
        P(),
        P(None, ("dp", "tensor"), None),
    )
    return jax.shard_map(
        on_device,
        mesh=mesh,
        in_specs=placed,
        out_specs=(
            P(None, ("dp", "tensor"), None),
            P(None, ("dp", "tensor"), None),
            P(None, "dp", "tensor"),
            P(None, "tensor"),
            P("tensor", "dp"),
            P(),
            P("dp", "tensor"),
            P("tensor"),
            P("tensor", "dp"),
            P(),
            P(),
            P(),
            P(),
            P(),
        ),
        check_vma=False,
    )
```

profile of v0, /device:TPU:0, one launch (start us, length us, event | category | flops | bytes accessed | tf_op | source)
XLA Modules:
  0.0 1003.8 jit_solution(3253380945306963484)
XLA Ops:
  16.1 14.6 %all_gather.25 = bf16[3,768,192]{2,0,1:T(4,128)(2,1)S(1)} all-gather(bf16[3,96,192]{2,0,1:T(4,128)(2,1)S(1)} %copy.45), channel_id=1, replica_groups=mesh['dp'=8,'tensor'=4] {'dp'}, dimensions={1}, use_global_device_ids=true | all-gather | bytes 995328 | tf_op jit(solution)/shard_map/all_gather | solution.py:179
  31.6 10.2 %all_gather.26 = bf16[192,768]{0,1:T(8,128)(2,1)} all-gather(bf16[192,96]{0,1:T(8,128)(2,1)S(1)} %copy.48), channel_id=1, replica_groups=mesh['dp'=8,'tensor'=4] {'dp'}, dimensions={1}, use_global_device_ids=true | all-gather | bytes 331776 | tf_op jit(solution)/shard_map/all_gather | solution.py:180
  47.7 33.4 %all-gather.8.cloned.1.call-done = bf16[2048,768]{1,0:T(8,128)(2,1)} async-done(((bf16[512,768]{1,0:T(8,128)(2,1)}), bf16[2048,768]{1,0:T(8,128)(2,1)}) %all-gather.8.cloned.1.call-update) | async-done | bytes 3145744 | tf_op jit(solution)/shard_map/all_gather | solution.py:128
  81.1 3.9 fusion.145
  118.0 3.7 fusion.146
  126.4 104.9 %reduce-scatter.11.cloned.1.call-done = f32[512,768]{1,0:T(8,128)} async-done(((f32[2048,768]{1,0:T(8,128)}), f32[512,768]{1,0:T(8,128)}) %reduce-scatter.11.cloned.1.call-update) | async-done | bytes 1572880 | tf_op jit(solution)/shard_map/reduce_scatter | solution.py:132
  238.8 61.3 %all-gather.10.cloned.1.call-done = bf16[2048,768]{1,0:T(8,128)(2,1)} async-done(((bf16[512,768]{1,0:T(8,128)(2,1)}), bf16[2048,768]{1,0:T(8,128)(2,1)}) %all-gather.10.cloned.1.call-update) | async-done | bytes 3145744 | tf_op jit(solution)/shard_map/all_gather | solution.py:128
  300.1 7.5 fusion.147
  307.6 16.8 %all-gather.14.cloned.1.call-done = bf16[768,768]{0,1:T(8,128)(2,1)} async-done(((bf16[768,96]{0,1:T(8,128)(2,1)}), bf16[768,768]{0,1:T(8,128)(2,1)}) %all-gather.14.cloned.1.call-update) | async-done | bytes 1179664 | tf_op jit(solution)/shard_map/all_gather | solution.py:184
  324.4 65.0 %all-gather.18.cloned.1.call-done = bf16[1,2048,768]{2,1,0:T(8,128)(2,1)} async-done(((bf16[1,512,768]{2,1,0:T(8,128)(2,1)}), bf16[1,2048,768]{2,1,0:T(8,128)(2,1)}) %all-gather.18.cloned.1.call-update) | async-done | bytes 3145744 | tf_op jit(solution)/shard_map/all_gather | solution.py:141
  389.4 9.4 convert_reduce_fusion
  400.5 4.6 fusion.148
  405.1 9.7 fusion.132
  416.6 97.9 %reduce-scatter.15.cloned.1.call-done = f32[512,768]{1,0:T(8,128)} async-done(((f32[2048,768]{1,0:T(8,128)}), f32[512,768]{1,0:T(8,128)}) %reduce-scatter.15.cloned.1.call-update) | async-done | bytes 1572880 | tf_op jit(solution)/shard_map/reduce_scatter | solution.py:145
  518.8 109.2 %reduce-scatter.13.cloned.1.call-done = f32[512,768]{1,0:T(8,128)} async-done(((f32[2048,768]{1,0:T(8,128)}), f32[512,768]{1,0:T(8,128)}) %reduce-scatter.13.cloned.1.call-update) | async-done | bytes 1572880 | tf_op jit(solution)/shard_map/reduce_scatter | solution.py:132
  628.0 4.8 fusion.133
  639.1 60.1 %all-gather.16.cloned.1.call-done = bf16[2048,768]{1,0:T(8,128)(2,1)} async-done(((bf16[512,768]{1,0:T(8,128)(2,1)}), bf16[2048,768]{1,0:T(8,128)(2,1)}) %all-gather.16.cloned.1.call-update) | async-done | bytes 3145744 | tf_op jit(solution)/shard_map/all_gather | solution.py:141
  711.3 7.8 multiply_reduce_fusion.2
  719.1 4.2 fusion.100
  723.4 6.3 multiply_reduce_fusion.1
  731.9 8.2 multiply_reduce_fusion
  752.1 5.3 multiply_convert_fusion.1
  759.9 6.5 multiply_convert_fusion
  781.0 7.2 convolution_bitcast_fusion
  788.2 6.8 convolution_convert_fusion.1
  795.0 3.9 all-to-all-start
  799.0 8.5 fusion.88
  807.5 13.5 %all-to-all-done = bf16[8,96,768]{2,1,0:T(8,128)(2,1)S(1)} async-done(((bf16[8,96,768]{2,1,0:T(8,128)(2,1)}), bf16[8,96,768]{2,1,0:T(8,128)(2,1)S(1)}, u32[]{:S(2)}, u32[]{:S(2)}) %all-to-all-start) | async-done | bytes 1179680 | tf_op jit(solution)/shard_map/all_to_all | solution.py:23
  821.0 3.6 all-to-all-start.1
  825.9 15.6 %all-to-all-done.1 = bf16[8,768,96]{1,2,0:T(8,128)(2,1)S(1)} async-done(((bf16[8,768,96]{1,2,0:T(8,128)(2,1)}), bf16[8,768,96]{1,2,0:T(8,128)(2,1)S(1)}, u32[]{:S(2)}, u32[]{:S(2)}) %all-to-all-start.1) | async-done | bytes 1179680 | tf_op jit(solution)/shard_map/all_to_all | solution.py:23
  849.3 98.4 %reduce-scatter.17.cloned.1.call-done = f32[512,768]{1,0:T(8,128)} async-done(((f32[2048,768]{1,0:T(8,128)}), f32[512,768]{1,0:T(8,128)}) %reduce-scatter.17.cloned.1.call-update) | async-done | bytes 1572880 | tf_op jit(solution)/shard_map/reduce_scatter | solution.py:145
  950.0 41.1 %psum.7 = f32[9216]{0:T(1024)S(1)} all-reduce(f32[9216]{0:T(1024)S(1)} %constant_dynamic-update-slice_fusion), channel_id=1, replica_groups=mesh['dp'=8,'tensor'=4] {'dp','tensor'}, use_global_device_ids=true, to_apply=%region_36.37 | all-reduce | flops 9216 | bytes 73728 | tf_op jit(solution)/shard_map/psum | solution.py:314
  (339 shorter events, 132.8 us)
Async XLA Ops:
  8.1 73.1 %all-gather.8.cloned.1.call-start = ((), (), s32[]{:S(2)}) async-start(), calls=%async_computation.8 | async-start | bytes 3932160 | tf_op jit(solution)/shard_map/all_gather | solution.py:128
  14.8 216.5 %reduce-scatter.11.cloned.1.call-start = ((), (), s32[]{:S(2)}) async-start(), calls=%async_computation.9 | async-start | bytes 7864320 | tf_op jit(solution)/shard_map/reduce_scatter | solution.py:132
  31.6 53.5 %copy-start.40 = (bf16[3,768,192]{1,2,0:T(8,128)(2,1)}, bf16[3,768,192]{1,2,0:T(8,128)(2,1)S(1)}, u32[]{:S(2)}) copy-start(bf16[3,768,192]{1,2,0:T(8,128)(2,1)S(1)} %copy.46) | copy-start | bytes 2654212
  85.2 21.1 %copy-start.10 = (bf16[1,2048,192]{1,2,0:T(8,128)(2,1)}, bf16[1,2048,192]{1,2,0:T(8,128)(2,1)S(1)}, u32[]{:S(2)}) copy-start(bf16[1,2048,192]{1,2,0:T(8,128)(2,1)S(1)} %slice.453) | copy-start | bytes 2359300
  85.3 12.4 %copy-start.16 = (bf16[1,1536,192]{1,2,0:T(8,128)(2,1)}, bf16[1,1536,192]{1,2,0:T(8,128)(2,1)S(1)}, u32[]{:S(2)}) copy-start(bf16[1,1536,192]{1,2,0:T(8,128)(2,1)S(1)} %slice.421) | copy-start | bytes 1769476
  87.1 14.0 %copy-start.23 = (bf16[1536,192]{0,1:T(8,128)(2,1)}, bf16[1536,192]{0,1:T(8,128)(2,1)S(1)}, u32[]{:S(2)}) copy-start(bf16[1536,192]{0,1:T(8,128)(2,1)S(1)} %slice.417) | copy-start | bytes 1769476
  121.7 117.1 %all-gather.12.cloned.1.call-start = ((), (), s32[]{:S(2)}) async-start(), calls=%async_computation.11 | async-start | bytes 1327104 | tf_op jit(solution)/shard_map/all_gather | solution.py:183
  122.3 177.8 %all-gather.10.cloned.1.call-start = ((), (), s32[]{:S(2)}) async-start(), calls=%async_computation.10 | async-start | bytes 3932160 | tf_op jit(solution)/shard_map/all_gather | solution.py:128
  236.2 88.3 %all-gather.14.cloned.1.call-start = ((), (), s32[]{:S(2)}) async-start(), calls=%async_computation.12 | async-start | bytes 1327104 | tf_op jit(solution)/shard_map/all_gather | solution.py:184
  236.7 152.7 %all-gather.18.cloned.1.call-start = ((), (), s32[]{:S(2)}) async-start(), calls=%async_computation.17 | async-start | bytes 3932160 | tf_op jit(solution)/shard_map/all_gather | solution.py:141
  237.5 277.0 %reduce-scatter.15.cloned.1.call-start = ((), (), s32[]{:S(2)}) async-start(), calls=%async_computation.14 | async-start | bytes 7864320 | tf_op jit(solution)/shard_map/reduce_scatter | solution.py:145
  389.4 11.0 %copy-start.83 = (bf16[768,768]{1,0:T(8,128)(2,1)S(1)}, bf16[768,768]{1,0:T(8,128)(2,1)}, u32[]{:S(2)}) copy-start(bf16[768,768]{1,0:T(8,128)(2,1)} %all-gather.12.cloned.1.call-done) | copy-start | bytes 3538948
  405.1 222.9 %reduce-scatter.13.cloned.1.call-start = ((), (), s32[]{:S(2)}) async-start(), calls=%async_computation.13 | async-start | bytes 7864320 | tf_op jit(solution)/shard_map/reduce_scatter | solution.py:132
  414.9 284.3 %all-gather.16.cloned.1.call-start = ((), (), s32[]{:S(2)}) async-start(), calls=%async_computation.15 | async-start | bytes 3932160 | tf_op jit(solution)/shard_map/all_gather | solution.py:141
  635.0 210.8 %reduce-scatter.21.cloned.1.call-start = ((), (), s32[]{:S(2)}) async-start(), calls=%async_computation.19 | async-start | bytes 884736
  710.0 137.3 %reduce-scatter.19.cloned.1.call-start = ((), (), s32[]{:S(2)}) async-start(), calls=%async_computation.18 | async-start | bytes 2211840
  711.3 12.1 %slice-start.3 = ((s8[9437184]{0:T(1024)(128)(4,1)}), s8[4194304]{0:T(1024)(128)(4,1)S(1)}, s32[]{:S(2)}) async-start(s8[9437184]{0:T(1024)(128)(4,1)} %bitcast.234), calls=%async_computation.23 | async-start | bytes 8388608
  711.3 12.1 %slice-start.4 = ((s8[9437184]{0:T(1024)(128)(4,1)}), s8[4194304]{0:T(1024)(128)(4,1)S(1)}, s32[]{:S(2)}) async-start(s8[9437184]{0:T(1024)(128)(4,1)} %bitcast.234), calls=%async_computation.24 | async-start | bytes 8388608
  780.9 166.7 %reduce-scatter.17.cloned.1.call-start = ((), (), s32[]{:S(2)}) async-start(), calls=%async_computation.16 | async-start | bytes 7864320 | tf_op jit(solution)/shard_map/reduce_scatter | solution.py:145
  788.2 10.8 %copy-start.80 = (f32[768]{0:T(1024)S(1)}, f32[768]{0:T(1024)}, u32[]{:S(2)}) copy-start(f32[768]{0:T(1024)} %convert_element_type.162) | copy-start | bytes 9220
  795.0 25.9 %all-to-all-start = ((bf16[8,96,768]{2,1,0:T(8,128)(2,1)}), bf16[8,96,768]{2,1,0:T(8,128)(2,1)S(1)}, u32[]{:S(2)}, u32[]{:S(2)}) async-start(bf16[8,96,768]{2,1,0:T(8,128)(2,1)} %bitcast.57), calls=%async_computation.4 | async-start | bytes 2359296 | tf_op jit(solution)/shard_map/all_to_all | solution.py:23
  799.0 25.6 %copy-start.13 = (bf16[1,512,768]{2,1,0:T(8,128)(2,1)S(1)}, bf16[1,512,768]{2,1,0:T(8,128)(2,1)}, u32[]{:S(2)}) copy-start(bf16[1,512,768]{2,1,0:T(8,128)(2,1)} %param.49) | copy-start | bytes 2359300
  807.5 17.3 %copy-start.81 = (f32[768]{0:T(1024)S(1)}, f32[768]{0:T(1024)}, u32[]{:S(2)}) copy-start(f32[768]{0:T(1024)} %get-tuple-element.219) | copy-start | bytes 9220
  821.0 20.6 %all-to-all-start.1 = ((bf16[8,768,96]{1,2,0:T(8,128)(2,1)}), bf16[8,768,96]{1,2,0:T(8,128)(2,1)S(1)}, u32[]{:S(2)}, u32[]{:S(2)}) async-start(bf16[8,768,96]{1,2,0:T(8,128)(2,1)} %bitcast.279), calls=%async_computation.5 | async-start | bytes 2359296 | tf_op jit(solution)/shard_map/all_to_all | solution.py:23
  824.7 122.9 %copy-start.4 = (bf16[1,512,768]{2,1,0:T(8,128)(2,1)S(1)}, bf16[1,512,768]{2,1,0:T(8,128)(2,1)}, u32[]{:S(2)}) copy-start(bf16[1,512,768]{2,1,0:T(8,128)(2,1)} %param.35) | copy-start | bytes 2359300
  824.7 122.9 %copy-start.56 = (f32[768]{0:T(1024)S(1)}, f32[768]{0:T(1024)}, u32[]{:S(2)}) copy-start(f32[768]{0:T(1024)} %copy-done.55) | copy-start | bytes 9220
  824.7 122.9 %copy-start.58 = (f32[512]{0:T(512)S(1)}, f32[512]{0:T(512)}, u32[]{:S(2)}) copy-start(f32[512]{0:T(512)} %copy-done.57) | copy-start | bytes 6148
  824.7 122.9 %copy-start.67 = (f32[512]{0:T(512)S(1)}, f32[512]{0:T(512)}, u32[]{:S(2)}) copy-start(f32[512]{0:T(512)} %copy-done.66) | copy-start | bytes 6148
  825.9 123.9 %copy-start.77 = (f32[768]{0:T(1024)S(1)}, f32[768]{0:T(1024)}, u32[]{:S(2)}) copy-start(f32[768]{0:T(1024)} %get-tuple-element.168) | copy-start | bytes 9220
  825.9 123.9 %copy-start.76 = (f32[768]{0:T(1024)S(1)}, f32[768]{0:T(1024)}, u32[]{:S(2)}) copy-start(f32[768]{0:T(1024)} %get-tuple-element.174) | copy-start | bytes 9220
  842.4 107.5 %copy-start.75 = (f32[768]{0:T(1024)S(1)}, f32[768]{0:T(1024)}, u32[]{:S(2)}) copy-start(f32[768]{0:T(1024)} %get-tuple-element.176) | copy-start | bytes 9220
  842.4 150.6 %copy-start.6 = (f32[512,768]{1,0:T(8,128)S(1)}, f32[512,768]{1,0:T(8,128)}, u32[]{:S(2)}) copy-start(f32[512,768]{1,0:T(8,128)} %copy-done.5) | copy-start | bytes 4718596
  (76 other events, 257.2 us)
Sparse Core Ops, SparseCore 0:
  14.9 66.1 all-gather.7
  121.8 109.3 reduce-scatter.10
  635.1 63.9 all-gather.15
Sparse Core Ops, SparseCore 1:
  124.1 22.5 all-gather.11
  236.2 63.8 all-gather.9
  301.9 22.5 all-gather.13
  326.0 63.3 all-gather.17
  405.2 109.3 reduce-scatter.14
  516.8 111.1 reduce-scatter.12
  710.1 33.6 reduce-scatter.20
  781.0 48.2 reduce-scatter.18
  831.5 116.0 reduce-scatter.16
where the time goes:
time: 1010 us; the launch traced here: 1000 us
  waiting for transfers between devices  678 us (67%)
  matrix products  131 us (13%)
  other arithmetic  68.9 us (7%)
  blocking collectives  65.9 us (7%)
  local copies, waits for them, and re-layouts  34 us (3%)
  between operations  17.1 us (2%)
    reduce_scatter x2, waiting for transfers between devices, rows_sum(): lax.psum_scatter(term_fn(jnp.int32(0), lax.axis_size('tensor') * row_coun...  214 us
    reduce_scatter x2, waiting for transfers between devices, grads_sum(): lax.psum_scatter(term_fn(jnp.int32(0), lax.axis_size('tensor') * row_coun...  196 us
    all_gather x2, waiting for transfers between devices, grads_gather(): return lax.all_gather(rows_low, 'tensor', axis=0, tiled=True)  125 us
    all_gather x2, waiting for transfers between devices, rows_gather(): return lax.all_gather(rows_low, 'tensor', axis=0, tiled=True)  94.8 us
    psum x1, blocking collectives, on_device(): summed = lax.psum(packed, ('dp', 'tensor'))  41.1 us
    all_to_all x2, waiting for transfers between devices, sum_at_owner(): lax.all_to_all(in_blocks(shard, dim, devices), axis, 0, 0, tiled=True)  29.1 us
    unnamed x202, local copies, waits for them, and re-layouts  25.5 us
    dot_general x4, matrix products, attend_backward(): jnp.einsum('qhe,khe->hqk', grad_block, values[:finish], preferred_element...  25.2 us
  transfers between devices with their start and end apart: 14, of which 11 were waited for; matrix products, arithmetic and copies ran while one was open for 14% of the time, Pallas kernels for 0%

commit v1 on v0

v1 whole, which is shorter than its diff:
```python
import jax
import jax.numpy as jnp
from jax import lax
from jax.sharding import PartitionSpec as P

HEAD_DIM = 64
EPSILON = 1e-05
MASKED = -1000000000.0
BF = jnp.bfloat16
F32 = jnp.float32


def norm_parts(row_vals):
    row_mean = jnp.mean(row_vals, axis=-1, keepdims=True)
    centred = row_vals - row_mean
    inverse = lax.rsqrt(jnp.mean(centred * centred, axis=-1, keepdims=True) + EPSILON)
    return (centred * inverse, inverse)


def norm_back(grad_normed, normed, inverse):
    first_mean = jnp.mean(grad_normed, axis=-1, keepdims=True)
    second_mean = jnp.mean(grad_normed * normed, axis=-1, keepdims=True)
    return inverse * (grad_normed - first_mean - normed * second_mean)


def doc_ids(pack_lengths, pack_len):
    seq_count = pack_lengths.shape[0]
    seq_ends = jnp.cumsum(pack_lengths, dtype=jnp.int32)
    places = jnp.arange(pack_len, dtype=jnp.int32)
    passed = jnp.sum(
        (places[:, None] >= seq_ends[None, :]).astype(jnp.int32), axis=1, dtype=jnp.int32
    )
    return jnp.where(passed < seq_count, passed, seq_count + places)


def allowed_block(doc_of, first_row, block_rows):
    finish = first_row + block_rows
    query_pos = jnp.arange(first_row, finish)
    key_pos = jnp.arange(finish)
    causal = key_pos[None, :] <= query_pos[:, None]
    return causal & (doc_of[first_row:finish, None] == doc_of[None, :finish])


def block_scores(query_block, key_rows, doc_of, first_row, block_rows, scale):
    finish = first_row + block_rows
    scores = (
        jnp.einsum("qhe,khe->hqk", query_block, key_rows[:finish], preferred_element_type=F32)
        * scale
    )
    return jnp.where(allowed_block(doc_of, first_row, block_rows)[None], scores, MASKED)


def attend_forward(queries, key_rows, values, doc_of, block_rows, scale):
    outputs, log_sums = ([], [])
    for first_row in range(0, queries.shape[0], block_rows):
        finish = first_row + block_rows
        scores = block_scores(
            queries[first_row:finish], key_rows, doc_of, first_row, block_rows, scale
        )
        row_max = jnp.max(scores, axis=-1, keepdims=True)
        exponent = jnp.exp(scores - row_max)
        row_total = jnp.sum(exponent, axis=-1, keepdims=True)
        attn_probs = (exponent / row_total).astype(BF)
        outputs.append(
            jnp.einsum("hqk,khe->qhe", attn_probs, values[:finish], preferred_element_type=F32)
        )
        log_sums.append(row_max + jnp.log(row_total))
    return (jnp.concatenate(outputs, axis=0), log_sums)


def attend_backward(queries, key_rows, values, grad_att, doc_of, log_sums, block_rows, scale):
    grad_queries = []
    grad_keys = jnp.zeros(key_rows.shape, F32)
    grad_values = jnp.zeros(values.shape, F32)
    for block_num, first_row in enumerate(range(0, queries.shape[0], block_rows)):
        finish = first_row + block_rows
        query_block = queries[first_row:finish]
        grad_block = grad_att[first_row:finish]
        scores = block_scores(query_block, key_rows, doc_of, first_row, block_rows, scale)
        attn_probs = jnp.exp(scores - log_sums[block_num])
        grad_probs = jnp.einsum(
            "qhe,khe->hqk", grad_block, values[:finish], preferred_element_type=F32
        )
        row_delta = jnp.sum(attn_probs * grad_probs, axis=-1, keepdims=True)
        grad_scores = (attn_probs * (grad_probs - row_delta)).astype(BF)
        grad_queries.append(
            scale
            * jnp.einsum(
                "hqk,khe->qhe", grad_scores, key_rows[:finish], preferred_element_type=F32
            )
        )
        grad_keys = grad_keys.at[:finish].add(
            scale
            * jnp.einsum("hqk,qhe->khe", grad_scores, query_block, preferred_element_type=F32)
        )
        grad_values = grad_values.at[:finish].add(
            jnp.einsum(
                "hqk,qhe->khe", attn_probs.astype(BF), grad_block, preferred_element_type=F32
            )
        )
    return (jnp.concatenate(grad_queries, axis=0), grad_keys, grad_values)


def dp_bits():
    return (lax.axis_size("dp") - 1).bit_length()


def doubles():
    size = lax.axis_size("dp")
    return size == 1 << dp_bits() and 1 < size <= 8


def relative_blocks():
    size = lax.axis_size("dp")
    pos = jnp.arange(size, dtype=jnp.int32)
    if not doubles():
        return pos
    high = dp_bits() - 1
    return ((pos & ((1 << high) - 1)) << 1 | pos >> high) ^ lax.axis_index("dp")


def chosen_columns(width):
    each = width // lax.axis_size("dp")
    source = (relative_blocks()[:, None] * each + jnp.arange(each, dtype=jnp.int32)).reshape(-1)
    return (jnp.arange(width, dtype=jnp.int32)[:, None] == source[None, :]).astype(BF)


def flip(value, axis, bit):
    size = lax.axis_size(axis)
    return lax.ppermute(value, axis, [(i, i ^ (1 << bit)) for i in range(size)])


def after(value, other):
    return lax.optimization_barrier((value, other))[0]


def line_steps(block):
    size = lax.axis_size("tensor")
    from_low, from_high = [], []
    going_up = going_down = block
    for step in range(size - 1):
        going_up = lax.ppermute(going_up, "tensor", [(i, i + 1) for i in range(step, size - 1)])
        going_down = lax.ppermute(
            going_down, "tensor", [(i + 1, i) for i in range(size - 1 - step)]
        )
        from_low.append(going_up)
        from_high.append(going_down)
    return from_low, from_high


def line_order(block, from_low, from_high):
    size = lax.axis_size("tensor")
    stacked = jnp.stack(from_low[::-1] + [block] + from_high)
    return lax.dynamic_slice_in_dim(stacked, size - 1 - lax.axis_index("tensor"), size, 0)


def line_sum(term):
    size = lax.axis_size("tensor")
    place = lax.axis_index("tensor")
    up = down = None
    for step in range(1, size):
        part_up = term(jnp.minimum(place + size - step, size - 1))
        part_down = term(jnp.maximum(place - size + step, 0))
        if up is not None:
            part_up = part_up + up.astype(F32)
            part_down = part_down + down.astype(F32)
        up = lax.ppermute(part_up.astype(BF), "tensor", [(i, i + 1) for i in range(step)])
        down = lax.ppermute(
            part_down.astype(BF), "tensor", [(size - 1 - i, size - 2 - i) for i in range(step)]
        )
    return term(place) + up.astype(F32) + down.astype(F32)


def exchange(blocks):
    size = lax.axis_size("tensor")
    place = lax.axis_index("tensor")
    result = jnp.zeros_like(blocks)
    own = lax.dynamic_index_in_dim(blocks, place, 0)
    result = lax.dynamic_update_slice_in_dim(result, own, place, 0)
    for shift in range(1, size):
        sent = lax.dynamic_index_in_dim(blocks, (place + shift) % size, 0)
        came = lax.ppermute(sent, "tensor", [(i, (i + shift) % size) for i in range(size)])
        result = lax.dynamic_update_slice_in_dim(result, came, (place - shift) % size, 0)
    return result


def doubled(block, upward):
    if not doubles():
        return lax.all_gather(block, "dp", axis=1)
    high = list(range(1, dp_bits()))
    shape = block.shape
    held = []
    for bit in high if upward else high[::-1]:
        came = flip(block, "dp", bit)
        at = 1 + sum(b > bit for b in held)
        block = jnp.stack([block, came], axis=at)
        held.append(bit)
    block = jnp.stack([block, flip(block, "dp", 0)], axis=1)
    return block.reshape(shape[0], lax.axis_size("dp"), *shape[1:])


def halved(parts, upward):
    if not doubles():
        return lax.psum_scatter(parts, "dp", scatter_dimension=1)
    bits = dp_bits()
    high = list(range(1, bits))
    parts = parts.reshape(parts.shape[0], *[2] * bits, *parts.shape[2:])
    axes = {0: 1, **{b: 1 + bits - b for b in high}}
    for bit in [0] + (high[::-1] if upward else high):
        at = axes[bit]
        keep = lax.index_in_dim(parts, 0, at, keepdims=False)
        came = flip(lax.index_in_dim(parts, 1, at, keepdims=False), "dp", bit)
        parts = (keep.astype(F32) + came.astype(F32)).astype(BF)
        axes = {b: a - (a > at) for b, a in axes.items()}
    return parts


def total(vector, axis):
    for bit in range((lax.axis_size(axis) - 1).bit_length()):
        vector = vector + flip(vector, axis, bit)
    return vector


def on_device(
    inputs,
    lengths,
    w_qkv,
    b_qv,
    w_out,
    b_out,
    w_fc,
    b_fc,
    w_proj,
    b_proj,
    gain_one,
    shift_one,
    gain_two,
    shift_two,
    cotangent,
):
    row_count, model_width = inputs.shape[1:]
    tensor_size = lax.axis_size("tensor")
    dp_size = lax.axis_size("dp")
    tensor_pos = lax.axis_index("tensor")
    pack_len = row_count * tensor_size
    head_width = w_qkv.shape[2]
    local_heads = head_width // HEAD_DIM
    block_rows = min(512, pack_len)
    scale = HEAD_DIM ** (-0.5)
    fc_local = b_fc.shape[0]
    owned = model_width // dp_size
    out_rows = owned * head_width // fc_local
    place = chosen_columns(model_width)

    def relative(rows):
        return jnp.dot(rows, place, preferred_element_type=F32)

    def absolute(rows):
        return jnp.einsum(
            "td,cd->tc",
            rows,
            place.astype(rows.dtype),
            precision=lax.Precision.HIGHEST,
            preferred_element_type=F32,
        )

    shard = jnp.concatenate([w_fc, w_proj.T, w_out.T.reshape(out_rows, fc_local), b_fc[None]])
    shard_low, shard_high = line_steps(shard)
    qkv_rows = jnp.concatenate([w_qkv[0], w_qkv[1], w_qkv[2]], axis=1)
    qkv_full = doubled(qkv_rows[None], True).reshape(model_width, 3 * head_width)

    vectors = relative(jnp.stack([gain_one, shift_one, gain_two, shift_two, b_out, b_proj]))
    gain_first, shift_first, gain_second, shift_second, bias_out, bias_proj = vectors
    rows_in = relative(inputs[0])
    normed_one, inverse_one = norm_parts(rows_in)
    h_one = (normed_one * gain_first + shift_first).astype(BF)
    h_one = after(h_one, (shard_low[-2], shard_high[-2]))
    h_one_all = line_order(h_one, *line_steps(h_one)).reshape(pack_len, model_width)

    shards = line_order(shard, shard_low, shard_high)
    cut = 2 * owned
    bias_fc = shards[:, -1:].astype(F32)
    some_out = jnp.concatenate([shards[:, :owned], shards[:, cut:-1]], axis=1)
    half_a = doubled(some_out, True)
    half_b = doubled(shards[:, owned:cut], False)
    fc_full = half_a[:, :, :owned].reshape(tensor_size, model_width, fc_local)
    out_t = half_a[:, :, owned:].reshape(tensor_size, model_width, head_width)
    proj_t = half_b.reshape(tensor_size, model_width, fc_local)

    doc_of = doc_ids(lengths[0, 0], pack_len)
    projected = jnp.dot(h_one_all, qkv_full, preferred_element_type=F32)
    projected = projected.reshape(pack_len, 3, local_heads, HEAD_DIM)
    bias_qv = b_qv.astype(F32).reshape(2, local_heads, HEAD_DIM)
    queries = (projected[:, 0] + bias_qv[0]).astype(BF)
    key_rows = projected[:, 1].astype(BF)
    values = (projected[:, 2] + bias_qv[1]).astype(BF)
    attended, log_sums = attend_forward(queries, key_rows, values, doc_of, block_rows, scale)
    att = exchange(attended.astype(BF).reshape(tensor_size, row_count, head_width))

    middle = (
        rows_in + jnp.einsum("ztc,zdc->td", att, out_t, preferred_element_type=F32) + bias_out
    )
    normed_two, inverse_two = norm_parts(middle)
    h_two = (normed_two * gain_second + shift_second).astype(BF)
    pre_act = jnp.einsum("td,zdf->ztf", h_two, fc_full, preferred_element_type=F32) + bias_fc
    root = (2.0 / jnp.pi) ** 0.5
    bend = jnp.tanh(root * (pre_act + 0.044715 * pre_act * pre_act * pre_act))
    active = (0.5 * pre_act * (1.0 + bend)).astype(BF)
    slope = 0.5 * (1.0 + bend) + 0.5 * pre_act * (1.0 - bend * bend) * root * (
        1.0 + 3 * 0.044715 * pre_act * pre_act
    )
    mlp_out = jnp.einsum("ztf,zdf->td", active, proj_t, preferred_element_type=F32)
    output = absolute((middle + mlp_out + bias_proj).astype(BF)).astype(BF)

    grad_y = relative(cotangent[0])
    grad_low = grad_y.astype(BF)
    grad_active = jnp.einsum("td,zdf->ztf", grad_low, proj_t, preferred_element_type=F32)
    grad_pre = (grad_active * slope).astype(BF)
    grad_h_two = jnp.einsum("ztf,zdf->td", grad_pre, fc_full, preferred_element_type=F32)
    grad_middle = grad_y + norm_back(grad_h_two * gain_second, normed_two, inverse_two)
    grad_branch = grad_middle.astype(BF)
    grad_att_rows = jnp.einsum("td,zdc->ztc", grad_branch, out_t, preferred_element_type=F32)
    heads_shape = (pack_len, local_heads, HEAD_DIM)
    grad_att = exchange(grad_att_rows.astype(BF)).reshape(heads_shape)

    def by_owner(left, right):
        full = jnp.einsum("td,ztf->zdf", left, right, preferred_element_type=F32).astype(BF)
        return full.reshape(tensor_size, dp_size, owned, right.shape[2])

    d_proj_all = by_owner(grad_low, active)
    d_fc_all = by_owner(h_two, grad_pre)
    d_out_all = by_owner(grad_branch, att).reshape(tensor_size, dp_size, out_rows, fc_local)
    part_a = halved(jnp.concatenate([d_fc_all, d_out_all], axis=2), True)
    part_b = halved(d_proj_all, False)
    shard_part = jnp.concatenate([part_a, part_b], axis=1)
    d_shard = line_sum(lambda j: lax.dynamic_index_in_dim(shard_part, j, 0, keepdims=False))
    d_fc = d_shard[:owned]
    d_out = d_shard[owned : owned + out_rows].reshape(owned, head_width).T
    d_proj = d_shard[owned + out_rows :].T

    early_rows = jnp.stack(
        [
            jnp.sum(grad_h_two * normed_two, axis=0),
            jnp.sum(grad_h_two, axis=0),
            jnp.sum(grad_middle, axis=0),
            jnp.sum(grad_y, axis=0),
        ]
    )
    early_fc = jnp.sum(grad_pre, axis=1, dtype=F32).reshape(-1)
    early = total(
        total(jnp.concatenate([absolute(early_rows).reshape(-1), early_fc]), "dp"), "tensor"
    )

    grad_query, grad_key, grad_value = attend_backward(
        queries, key_rows, values, grad_att, doc_of, log_sums, block_rows, scale
    )
    stacked = jnp.concatenate(
        [g.reshape(pack_len, head_width) for g in (grad_query, grad_key, grad_value)], axis=1
    ).astype(BF)
    sums = jnp.sum(stacked, axis=0, dtype=F32)
    sum_qv = jnp.stack([sums[:head_width], sums[2 * head_width :]])

    def input_term(j):
        mine = lax.dynamic_slice_in_dim(stacked, j * row_count, row_count, 0)
        return jnp.einsum("te,de->td", mine, qkv_full, preferred_element_type=F32)

    grad_h_one = line_sum(input_term)
    qkv_all = jnp.einsum("td,te->de", h_one_all, stacked, preferred_element_type=F32).astype(BF)
    d_qkv = halved(qkv_all.reshape(1, dp_size, owned, 3 * head_width), True)[0]
    d_qkv = d_qkv.astype(F32).reshape(owned, 3, head_width).transpose(1, 0, 2)

    grad_in = absolute(
        grad_middle + norm_back(grad_h_one * gain_first, normed_one, inverse_one)
    )
    late_rows = jnp.stack([jnp.sum(grad_h_one * normed_one, axis=0), jnp.sum(grad_h_one, axis=0)])
    late = total(
        jnp.concatenate([absolute(late_rows).reshape(-1), sum_qv.reshape(-1)]), "dp"
    )
    wide = model_width
    sum_qv = late[2 * wide :].reshape(2, head_width)
    late = total(late[: 2 * wide], "tensor")
    d_b_fc = lax.dynamic_slice(early[4 * wide :], (tensor_pos * fc_local,), (fc_local,))
    return (
        output[None],
        grad_in[None],
        d_qkv,
        sum_qv,
        d_out,
        early[2 * wide : 3 * wide],
        d_fc,
        d_b_fc,
        d_proj,
        early[3 * wide : 4 * wide],
        late[:wide],
        late[wide:],
        early[:wide],
        early[wide : 2 * wide],
    )


def solution(mesh):
    rows = P(None, ("dp", "tensor"), None)
    placed = (
        rows,
        P("dp", None, None),
        P(None, "dp", "tensor"),
        P(None, "tensor"),
        P("tensor", "dp"),
        P(),
        P("dp", "tensor"),
        P("tensor"),
        P("tensor", "dp"),
        P(),
        P(),
        P(),
        P(),
        P(),
        rows,
    )
    return jax.shard_map(
        on_device,
        mesh=mesh,
        in_specs=placed,
        out_specs=(
            rows,
            rows,
            P(None, "dp", "tensor"),
            P(None, "tensor"),
            P("tensor", "dp"),
            P(),
            P("dp", "tensor"),
            P("tensor"),
            P("tensor", "dp"),
            P(),
            P(),
            P(),
            P(),
            P(),
        ),
        check_vma=False,
    )
```

time: 1010 us -> 534 us (0.53)
  waiting for transfers between devices: 678 us -> 132 us
  starting transfers between devices: 8.63 us -> 93.9 us
  blocking collectives: 65.9 us -> 0 us
  local copies, waits for them, and re-layouts: 34 us -> 86.2 us
  between operations: 17.1 us -> 3.25 us
  other arithmetic: 68.9 us -> 82.6 us
    reduce_scatter x4 -> x0, waiting for transfers between devices: 410 us -> none  [the longest x2 214 us: rows_sum(): lax.psum_scatter(term_fn(jnp.int32(0), lax.axis_size('tensor') * row_coun...]
    all_gather x6 -> x0, waiting for transfers between devices: 237 us -> none  [the longest x2 125 us: grads_gather(): return lax.all_gather(rows_low, 'tensor', axis=0, tiled=True)]
    ppermute x0 -> x58, waiting for transfers between devices: none -> 132 us  [the longest x28 61.9 us: flip(): return lax.ppermute(value, axis, [(i, i ^ 1 << bit) for i in range(size)])]
    ppermute x0 -> x58, starting transfers between devices: none -> 93.9 us  [the longest x6 29.7 us: line_sum(): lax.ppermute(part_up.astype(BF), 'tensor', [(i, i + 1) for i in range(ste...]
    psum x1 -> x0, blocking collectives: 41.1 us -> none  [on_device(): summed = lax.psum(packed, ('dp', 'tensor'))]
    all_to_all x2 -> x0, waiting for transfers between devices: 29.1 us -> none  [sum_at_owner(): lax.all_to_all(in_blocks(shard, dim, devices), axis, 0, 0, tiled=True)]
    all_gather x2 -> x0, blocking collectives: 24.8 us -> none  [the longest x1 14.6 us: on_device(): lax.all_gather(w_qkv, 'dp', axis=1, tiled=True)]
    another operation x3 -> x13, other arithmetic: 3.27 us -> 23.3 us  [the longest x6 13 us: doubled(): block = jnp.stack([block, flip(block, 'dp', 0)], axis=1)]
  transfers between devices with their start and end apart: 14 -> 58, of which waited for: 11 -> 21; matrix products, arithmetic and copies ran while one was open for 14% -> 43% of each run, Pallas kernels for 0% -> 0%
where the time goes in v1:
time: 534 us; the launch traced here: 523 us
  waiting for transfers between devices  132 us (25%)
  matrix products  126 us (24%)
  starting transfers between devices  93.9 us (18%)
  local copies, waits for them, and re-layouts  86.2 us (16%)
  other arithmetic  82.6 us (15%)
    ppermute x28, waiting for transfers between devices, flip(): return lax.ppermute(value, axis, [(i, i ^ 1 << bit) for i in range(size)])  61.9 us
    ppermute x6, waiting for transfers between devices, line_sum(): lax.ppermute(part_up.astype(BF), 'tensor', [(i, i + 1) for i in range(ste...  32.2 us
    ppermute x6, starting transfers between devices, line_sum(): lax.ppermute(part_up.astype(BF), 'tensor', [(i, i + 1) for i in range(ste...  29.7 us
    unnamed x190, local copies, waits for them, and re-layouts  28.8 us
    ppermute x28, starting transfers between devices, flip(): return lax.ppermute(value, axis, [(i, i ^ 1 << bit) for i in range(size)])  27.7 us
    ppermute x6, waiting for transfers between devices, line_steps(): lax.ppermute(going_down, 'tensor', [(i + 1, i) for i in range(size - 1 -...  20 us
    convert_element_type x4, other arithmetic, attend_backward(): grad_scores = (attn_probs * (grad_probs - row_delta)).astype(BF)  17.9 us
    dot_general x4, matrix products, attend_backward(): jnp.einsum('qhe,khe->hqk', grad_block, values[:finish], preferred_element...  16.7 us
  transfers between devices with their start and end apart: 58, of which 21 were waited for; matrix products, arithmetic and copies ran while one was open for 43% of the time, Pallas kernels for 0%

profile of v1, /device:TPU:0, one launch (start us, length us, event | category | flops | bytes accessed | tf_op | source)
XLA Modules:
  0.0 523.3 jit_solution(2150521406698716269)
XLA Ops:
  4.7 5.6 %collective-permute-start = (bf16[217,768]{1,0:T(8,128)(2,1)S(1)}, bf16[217,768]{1,0:T(8,128)(2,1)S(1)}, u32[]{:S(2)}, u32[]{:S(2)}) collective-permute-start(bf16[217,768]{1,0:T(8,128)(2,1)S(1)} %pad_maximum_fusion.13), channel_id=1, source_target_pairs={{0,1},{1,2},{2,3},{4,5},{5,6},{6,7},{8,9},{9,10},{10,11},{12,13},{... | collective-permute-start | bytes 999944 | tf_op jit(solution)/shard_map/ppermute | solution.py:142
  26.8 10.6 %collective-permute-done.3 = bf16[217,768]{1,0:T(8,128)(2,1)} collective-permute-done((bf16[217,768]{1,0:T(8,128)(2,1)}, bf16[217,768]{1,0:T(8,128)(2,1)}, u32[]{:S(2)}, u32[]{:S(2)}) %collective-permute-start.3) | collective-permute-done | bytes 333344 | tf_op jit(solution)/shard_map/ppermute | solution.py:143
  37.4 4.5 collective-permute-start.4
  83.8 25.2 %collective-permute-done.18 = bf16[4,120,768]{2,1,0:T(8,128)(2,1)} collective-permute-done((bf16[4,120,768]{2,1,0:T(8,128)(2,1)}, bf16[4,120,768]{2,1,0:T(8,128)(2,1)}, u32[]{:S(2)}, u32[]{:S(2)}) %collective-permute-start.18) | collective-permute-done | bytes 737312 | tf_op jit(solution)/shard_map/ppermute | solution.py:130
  124.5 5.3 %collective-permute-done.9 = bf16[512,768]{0,1:T(8,128)(2,1)S(1)} collective-permute-done((bf16[512,768]{0,1:T(8,128)(2,1)}, bf16[512,768]{0,1:T(8,128)(2,1)S(1)}, u32[]{:S(2)}, u32[]{:S(2)}) %collective-permute-start.9) | collective-permute-done | bytes 786464 | tf_op jit(solution)/shard_map/ppermute | solution.py:143
  131.7 4.9 copy.104
  143.4 5.6 %fusion.243 = (f32[3,512]{1,0:T(4,128)S(1)}, f32[3,512,1536]{2,1,0:T(8,128)}) fusion(bf16[2048,3,3,64]{0,3,2,1:T(8,128)(2,1)S(1)} %get-tuple-element.236, bf16[2048,3,64]{0,2,1:T(8,128)(2,1)S(1)} %get-tuple-element.180, pred[512,1536]{1,0:T(8,128)(4,1)S(1)} %copy-done.40), kind=kOutput, calls=%fused_computation.427 | convolution fusion | flops 309066240 | bytes 11016192 | tf_op jit(solution)/shard_map/qhe,khe->hqk/dot_general | solution.py:47
  160.1 5.1 fusion.2
  165.2 5.6 %fusion.132 = bf16[512,3,64]{0,2,1:T(8,128)(2,1)S(1)} fusion(f32[3,512,1536]{2,1,0:T(8,128)} %get-tuple-element.241, f32[3,512]{1,0:T(4,128)S(1)} %fusion.2, f32[3,512]{1,0:T(4,128)S(1)} %get-tuple-element.240, bf16[2048,3,64]{0,2,1:T(8,128)(2,1)S(1)} %get-tuple-element.181), kind=kOutput, calls=%fused_computation.216 | convolution fusion | flops 309166080 | bytes 10240000 | tf_op jit(solution)/shard_map/hqk,khe->qhe/dot_general | solution.py:65
  193.3 7.5 %collective-permute-done.14 = bf16[1,512,192]{1,2,0:T(8,128)(2,1)S(1)} collective-permute-done((bf16[1,512,192]{1,2,0:T(8,128)(2,1)S(1)}, bf16[1,512,192]{1,2,0:T(8,128)(2,1)S(1)}, u32[]{:S(2)}, u32[]{:S(2)}) %collective-permute-start.14) | collective-permute-done | bytes 196640 | tf_op jit(solution)/shard_map/ppermute | solution.py:182
  217.3 5.2 fusion.225
  222.6 4.7 convolution_convert_fusion
  227.3 6.6 %convert_reduce_fusion = (f32[4,768]{1,0:T(4,128)S(1)}, bf16[4,512,768]{2,1,0:T(8,128)(2,1)S(1)}) fusion(f32[4,768,512]{1,2,0:T(8,128)S(1)} %fusion.225, f32[4,768]{1,0:T(4,128)S(1)} %bitcast.484, bf16[4,768,768]{2,1,0:T(8,128)(2,1)S(1)} %bitcast.450, f32[768,512]{1,0:T(8,128)S(1)} %copy-done.19), kind=kOutput, calls=%fused_computation.27 | convolution fusion | flops 2450912256 | bytes 15753216 | tf_op jit(solution)/shard_map/td,zdf->ztf/dot_general | solution.py:317
  237.7 4.7 convolution_convert_fusion.1
  246.1 4.9 fusion.234
  318.0 5.7 %multiply_reduce_fusion.1 = (f32[3,512]{1,0:T(4,128)S(1)}, f32[3,512,1536]{2,1,0:T(8,128)}) fusion(f32[3,512,1536]{2,1,0:T(8,128)S(1)} %bitcast.435, f32[3,512]{1,0:T(4,128)S(1)} %log_add_fusion.1, bf16[512,3,64]{0,2,1:T(8,128)(2,1)S(1)} %bitcast.467, bf16[2048,3,64]{0,2,1:T(8,128)(2,1)S(1)} %get-tuple-element.181), kind=kOutput, calls=%fused_computation.11 | convolution fusion | flops 309066240 | bytes 19675136 | tf_op jit(solution)/shard_map/qhe,khe->hqk/dot_general | solution.py:81
  326.0 6.3 %multiply_reduce_fusion = (f32[3,512]{1,0:T(4,128)S(1)}, f32[3,512,2048]{2,1,0:T(8,128)}) fusion(f32[3,512,2048]{2,1,0:T(8,128)S(1)} %bitcast.433, f32[3,512]{1,0:T(4,128)S(1)} %log_add_fusion, bf16[512,3,64]{0,2,1:T(8,128)(2,1)S(1)} %bitcast.465, bf16[2048,3,64]{0,2,1:T(8,128)(2,1)S(1)} %get-tuple-element.181), kind=kOutput, calls=%fused_computation.1 | convolution fusion | flops 412088832 | bytes 26161152 | tf_op jit(solution)/shard_map/qhe,khe->hqk/dot_general | solution.py:81
  334.6 5.5 %multiply_convert_fusion.2 = bf16[3,512,1024]{2,1,0:T(8,128)(2,1)S(1)} fusion(f32[3,512,1024]{2,1,0:T(8,128)} %get-tuple-element.251, f32[3,512,1024]{2,1,0:T(8,128)} %copy-done.3, f32[3,512]{1,0:T(4,128)S(1)} %get-tuple-element.250, f32[3,512]{1,0:T(4,128)S(1)} %copy-done.48), kind=kLoop, calls=%fused_computation.29 | loop fusion | flops 6291456 | bytes 15740928 | tf_op jit(solution)/shard_map/convert_element_type | solution.py:85
  343.0 5.2 %multiply_convert_fusion.1 = bf16[3,512,1536]{2,1,0:T(8,128)(2,1)S(1)} fusion(f32[3,512,1536]{2,1,0:T(8,128)} %get-tuple-element.253, f32[3,512,1536]{2,1,0:T(8,128)S(1)} %bitcast.435, f32[3,512]{1,0:T(4,128)S(1)} %get-tuple-element.252, f32[3,512]{1,0:T(4,128)S(1)} %log_add_fusion.1), kind=kLoop, calls=%fused_computation.10 | loop fusion | flops 9437184 | bytes 23605248 | tf_op jit(solution)/shard_map/convert_element_type | solution.py:85
  351.8 6.3 %multiply_convert_fusion = bf16[3,512,2048]{2,1,0:T(8,128)(2,1)S(1)} fusion(f32[3,512,2048]{2,1,0:T(8,128)} %get-tuple-element.255, f32[3,512,2048]{2,1,0:T(8,128)S(1)} %bitcast.433, f32[3,512]{1,0:T(4,128)S(1)} %get-tuple-element.254, f32[3,512]{1,0:T(4,128)S(1)} %log_add_fusion), kind=kLoop, calls=%fused_computation | loop fusion | flops 12582912 | bytes 31469568 | tf_op jit(solution)/shard_map/convert_element_type | solution.py:85
  380.6 9.8 %collective-permute-done.27 = bf16[512,768]{0,1:T(8,128)(2,1)} collective-permute-done((bf16[512,768]{0,1:T(8,128)(2,1)}, bf16[512,768]{0,1:T(8,128)(2,1)}, u32[]{:S(2)}, u32[]{:S(2)}) %collective-permute-start.27) | collective-permute-done | bytes 786464 | tf_op jit(solution)/shard_map/ppermute | solution.py:167
  392.5 4.6 collective-permute-start.28
  400.7 12.7 %collective-permute-done.28 = bf16[512,768]{0,1:T(8,128)(2,1)S(1)} collective-permute-done((bf16[512,768]{0,1:T(8,128)(2,1)S(1)}, bf16[512,768]{0,1:T(8,128)(2,1)S(1)}, u32[]{:S(2)}, u32[]{:S(2)}) %collective-permute-start.28) | collective-permute-done | bytes 786464 | tf_op jit(solution)/shard_map/ppermute | solution.py:167
  414.2 4.6 collective-permute-start.29
  428.9 5.4 %collective-permute-done.29 = bf16[512,768]{0,1:T(8,128)(2,1)S(1)} collective-permute-done((bf16[512,768]{0,1:T(8,128)(2,1)S(1)}, bf16[512,768]{0,1:T(8,128)(2,1)S(1)}, u32[]{:S(2)}, u32[]{:S(2)}) %collective-permute-start.29) | collective-permute-done | bytes 786464 | tf_op jit(solution)/shard_map/ppermute | solution.py:167
  434.2 5.0 collective-permute-done.32
  441.1 8.7 %collective-permute-done.43 = bf16[4,2,96,768]{3,2,0,1:T(8,128)(2,1)S(1)} collective-permute-done((bf16[4,2,96,768]{3,2,0,1:T(8,128)(2,1)S(1)}, bf16[4,2,96,768]{3,2,0,1:T(8,128)(2,1)S(1)}, u32[]{:S(2)}, u32[]{:S(2)}) %collective-permute-start.43) | collective-permute-done | bytes 1179680 | tf_op jit(solution)/shard_map/ppermute | solution.py:130
  450.7 12.0 %collective-permute-done.40 = bf16[4,2,120,768]{3,2,0,1:T(8,128)(2,1)S(1)} collective-permute-done((bf16[4,2,120,768]{3,2,0,1:T(8,128)(2,1)S(1)}, bf16[4,2,120,768]{3,2,0,1:T(8,128)(2,1)S(1)}, u32[]{:S(2)}, u32[]{:S(2)}) %collective-permute-start.40) | collective-permute-done | bytes 1474592 | tf_op jit(solution)/shard_map/ppermute | solution.py:130
  473.6 4.7 collective-permute-done.41
  496.7 4.6 collective-permute-start.57
  503.6 8.5 %collective-permute-start.47 = (bf16[216,768]{1,0:T(8,128)(2,1)S(1)}, bf16[216,768]{1,0:T(8,128)(2,1)S(1)}, u32[]{:S(2)}, u32[]{:S(2)}) collective-permute-start(bf16[216,768]{1,0:T(8,128)(2,1)S(1)} %get-tuple-element.190), channel_id=1, source_target_pairs={{0,1},{1,2},{2,3},{4,5},{5,6},{6,7},{8,9},{9,10},{10,11},{12,13},{... | collective-permute-start | bytes 995336 | tf_op jit(solution)/shard_map/ppermute | solution.py:167
  513.7 5.5 %fusion.82 = f32[1,512,768]{2,1,0:T(8,128)} fusion(f32[512,768]{0,1:T(8,128)S(1)} %copy-done.9, f32[512,768]{0,1:T(8,128)S(1)} %copy-done.36, s32[768]{0:T(1024)S(1)} %copy-done.61, f32[768,512]{1,0:T(8,128)S(1)} %copy-done.7, f32[512]{0:T(512)S(1)} %broadcast_multiply_fusion, f32[512]{0:T(512)S(1)} %broadcast_multiply_fusion.1, f32[768]{0:T(1024)S(1)} %copy-done.52, ...), kind=kOutput, calls=%fused_computation.156 | convolution fusion | flops 3627614208 | bytes 6305792 | tf_op jit(solution)/shard_map/td,cd->tc/dot_general | solution.py:259
  (492 shorter events, 299.2 us)
Async XLA Ops:
  3.4 19.7 %collective-permute-start.2 = (bf16[217,768]{1,0:T(8,128)(2,1)S(1)}, bf16[217,768]{1,0:T(8,128)(2,1)}, u32[]{:S(2)}, u32[]{:S(2)}) collective-permute-start(bf16[217,768]{1,0:T(8,128)(2,1)S(1)} %pad_maximum_fusion.13), channel_id=1, source_target_pairs={{1,0},{2,1},{3,2},{5,4},{6,5},{7,6},{9,8},{10,9},{11,10},{13,12},{... | collective-permute-start | bytes 999944 | tf_op jit(solution)/shard_map/ppermute | solution.py:143
  12.0 52.6 %collective-permute-start.10 = (bf16[1,96,576]{2,1,0:T(8,128)(2,1)}, bf16[1,96,576]{2,1,0:T(8,128)(2,1)}, u32[]{:S(2)}, u32[]{:S(2)}) collective-permute-start(bf16[1,96,576]{2,1,0:T(8,128)(2,1)} %get-tuple-element.218), channel_id=1, source_target_pairs={{0,8},{4,12},{8,0},{12,4},{16,24},{20,28},{24,16},{28,20},{1,9},{5... | collective-permute-start | bytes 331784 | tf_op jit(solution)/shard_map/ppermute | solution.py:130
  24.5 18.8 %collective-permute-start.16 = (bf16[217,768]{1,0:T(8,128)(2,1)}, bf16[217,768]{1,0:T(8,128)(2,1)}, u32[]{:S(2)}, u32[]{:S(2)}) collective-permute-start(bf16[217,768]{1,0:T(8,128)(2,1)} %collective-permute-done.1), channel_id=1, source_target_pairs={{2,3},{6,7},{10,11},{14,15},{18,19},{22,23},{26,27},{30,31}} | collective-permute-start | bytes 999944 | tf_op jit(solution)/shard_map/ppermute | solution.py:142
  37.4 25.6 %collective-permute-start.4 = (bf16[512,768]{0,1:T(8,128)(2,1)S(1)}, bf16[512,768]{0,1:T(8,128)(2,1)}, u32[]{:S(2)}, u32[]{:S(2)}) collective-permute-start(bf16[512,768]{0,1:T(8,128)(2,1)S(1)} %add_convert_fusion.5), channel_id=1, source_target_pairs={{0,1},{1,2},{2,3},{4,5},{5,6},{6,7},{8,9},{9,10},{10,11},{12,13},{... | collective-permute-start | bytes 2359304 | tf_op jit(solution)/shard_map/ppermute | solution.py:142
  57.6 18.2 %collective-permute-start.7 = (bf16[512,768]{0,1:T(8,128)(2,1)S(1)}, bf16[512,768]{0,1:T(8,128)(2,1)}, u32[]{:S(2)}, u32[]{:S(2)}) collective-permute-start(bf16[512,768]{0,1:T(8,128)(2,1)S(1)} %add_convert_fusion.5), channel_id=1, source_target_pairs={{1,0},{2,1},{3,2},{5,4},{6,5},{7,6},{9,8},{10,9},{11,10},{13,12},{... | collective-permute-start | bytes 2359304 | tf_op jit(solution)/shard_map/ppermute | solution.py:143
  70.6 44.1 %collective-permute-start.22 = (bf16[4,2,96,768]{3,2,0,1:T(8,128)(2,1)}, bf16[4,2,96,768]{3,2,0,1:T(8,128)(2,1)}, u32[]{:S(2)}, u32[]{:S(2)}) collective-permute-start(bf16[4,2,96,768]{3,2,0,1:T(8,128)(2,1)} %get-tuple-element.197), channel_id=1, source_target_pairs={{0,8},{4,12},{8,0},{12,4},{16,24},{20,28},{24,16},{28,20},{1,9},{5... | collective-permute-start | bytes 3538952 | tf_op jit(solution)/shard_map/ppermute | solution.py:130
  74.1 34.9 %collective-permute-start.18 = (bf16[4,120,768]{2,1,0:T(8,128)(2,1)}, bf16[4,120,768]{2,1,0:T(8,128)(2,1)}, u32[]{:S(2)}, u32[]{:S(2)}) collective-permute-start(bf16[4,120,768]{2,1,0:T(8,128)(2,1)} %get-tuple-element.210), channel_id=1, source_target_pairs={{0,8},{4,12},{8,0},{12,4},{16,24},{20,28},{24,16},{28,20},{1,9},{5... | collective-permute-start | bytes 2211848 | tf_op jit(solution)/shard_map/ppermute | solution.py:130
  75.7 37.6 %collective-permute-start.8 = (bf16[512,768]{0,1:T(8,128)(2,1)}, bf16[512,768]{0,1:T(8,128)(2,1)}, u32[]{:S(2)}, u32[]{:S(2)}) collective-permute-start(bf16[512,768]{0,1:T(8,128)(2,1)} %collective-permute-done.7), channel_id=1, source_target_pairs={{1,0},{2,1},{5,4},{6,5},{9,8},{10,9},{13,12},{14,13},{17,16},{18,1... | collective-permute-start | bytes 2359304 | tf_op jit(solution)/shard_map/ppermute | solution.py:143
  78.3 40.0 %collective-permute-start.6 = (bf16[512,768]{0,1:T(8,128)(2,1)}, bf16[512,768]{0,1:T(8,128)(2,1)}, u32[]{:S(2)}, u32[]{:S(2)}) collective-permute-start(bf16[512,768]{0,1:T(8,128)(2,1)} %collective-permute-done.5), channel_id=1, source_target_pairs={{2,3},{6,7},{10,11},{14,15},{18,19},{22,23},{26,27},{30,31}} | collective-permute-start | bytes 2359304 | tf_op jit(solution)/shard_map/ppermute | solution.py:142
  111.8 59.0 %collective-permute-start.19 = (bf16[4,2,120,768]{3,2,0,1:T(8,128)(2,1)}, bf16[4,2,120,768]{3,2,0,1:T(8,128)(2,1)}, u32[]{:S(2)}, u32[]{:S(2)}) collective-permute-start(bf16[4,2,120,768]{3,2,0,1:T(8,128)(2,1)} %get-tuple-element.189), channel_id=1, source_target_pairs={{0,16},{4,20},{8,24},{12,28},{16,0},{20,4},{24,8},{28,12},{1,17},{... | collective-permute-start | bytes 4423688 | tf_op jit(solution)/shard_map/ppermute | solution.py:130
  118.4 82.4 %collective-permute-start.23 = (bf16[4,2,2,96,768]{4,3,0,1,2:T(8,128)(2,1)}, bf16[4,2,2,96,768]{4,3,0,1,2:T(8,128)(2,1)}, u32[]{:S(2)}, u32[]{:S(2)}) collective-permute-start(bf16[4,2,2,96,768]{4,3,0,1,2:T(8,128)(2,1)} %get-tuple-element.187), channel_id=1, source_target_pairs={{0,4},{4,0},{8,12},{12,8},{16,20},{20,16},{24,28},{28,24},{1,5},{5... | collective-permute-start | bytes 7077896 | tf_op jit(solution)/shard_map/ppermute | solution.py:130
  175.2 30.6 %collective-permute-start.20 = (bf16[4,2,2,120,768]{4,3,0,2,1:T(8,128)(2,1)}, bf16[4,2,2,120,768]{4,3,0,2,1:T(8,128)(2,1)}, u32[]{:S(2)}, u32[]{:S(2)}) collective-permute-start(bf16[4,2,2,120,768]{4,3,0,2,1:T(8,128)(2,1)} %get-tuple-element.183), channel_id=1, source_target_pairs={{0,4},{4,0},{8,12},{12,8},{16,20},{20,16},{24,28},{28,24},{1,5},{5... | collective-permute-start | bytes 8847368 | tf_op jit(solution)/shard_map/ppermute | solution.py:130
  183.6 17.1 %collective-permute-start.14 = (bf16[1,512,192]{1,2,0:T(8,128)(2,1)S(1)}, bf16[1,512,192]{1,2,0:T(8,128)(2,1)S(1)}, u32[]{:S(2)}, u32[]{:S(2)}) collective-permute-start(bf16[1,512,192]{1,2,0:T(8,128)(2,1)S(1)} %copy.175), channel_id=1, source_target_pairs={{0,2},{1,3},{2,0},{3,1},{4,6},{5,7},{6,4},{7,5},{8,10},{9,11},{10,... | collective-permute-start | bytes 589832 | tf_op jit(solution)/shard_map/ppermute | solution.py:182
  280.0 24.1 %collective-permute-start.26 = (bf16[1,512,192]{1,2,0:T(8,128)(2,1)}, bf16[1,512,192]{1,2,0:T(8,128)(2,1)}, u32[]{:S(2)}, u32[]{:S(2)}) collective-permute-start(bf16[1,512,192]{1,2,0:T(8,128)(2,1)} %get-tuple-element.202), channel_id=1, source_target_pairs={{0,3},{1,0},{2,1},{3,2},{4,7},{5,4},{6,5},{7,6},{8,11},{9,8},{10,9... | collective-permute-start | bytes 589832 | tf_op jit(solution)/shard_map/ppermute | solution.py:182
  280.5 22.1 %collective-permute-start.25 = (bf16[1,512,192]{1,2,0:T(8,128)(2,1)}, bf16[1,512,192]{1,2,0:T(8,128)(2,1)}, u32[]{:S(2)}, u32[]{:S(2)}) collective-permute-start(bf16[1,512,192]{1,2,0:T(8,128)(2,1)} %get-tuple-element.203), channel_id=1, source_target_pairs={{0,2},{1,3},{2,0},{3,1},{4,6},{5,7},{6,4},{7,5},{8,10},{9,11},{10,... | collective-permute-start | bytes 589832 | tf_op jit(solution)/shard_map/ppermute | solution.py:182
  281.5 19.4 %collective-permute-start.24 = (bf16[1,512,192]{1,2,0:T(8,128)(2,1)}, bf16[1,512,192]{1,2,0:T(8,128)(2,1)}, u32[]{:S(2)}, u32[]{:S(2)}) collective-permute-start(bf16[1,512,192]{1,2,0:T(8,128)(2,1)} %get-tuple-element.204), channel_id=1, source_target_pairs={{0,1},{1,2},{2,3},{3,0},{4,5},{5,6},{6,7},{7,4},{8,9},{9,10},{10,1... | collective-permute-start | bytes 589832 | tf_op jit(solution)/shard_map/ppermute | solution.py:182
  290.3 130.6 %collective-permute-start.42 = (bf16[4,2,2,96,768]{4,3,0,1,2:T(8,128)(2,1)}, bf16[4,2,2,96,768]{4,3,0,1,2:T(8,128)(2,1)}, u32[]{:S(2)}, u32[]{:S(2)}) collective-permute-start(bf16[4,2,2,96,768]{4,3,0,1,2:T(8,128)(2,1)} %bitcast.428), channel_id=1, source_target_pairs={{0,4},{4,0},{8,12},{12,8},{16,20},{20,16},{24,28},{28,24},{1,5},{5... | collective-permute-start | bytes 7077896 | tf_op jit(solution)/shard_map/ppermute | solution.py:130
  299.4 125.4 %collective-permute-start.39 = (bf16[4,2,2,120,768]{4,3,0,2,1:T(8,128)(2,1)}, bf16[4,2,2,120,768]{4,3,0,2,1:T(8,128)(2,1)}, u32[]{:S(2)}, u32[]{:S(2)}) collective-permute-start(bf16[4,2,2,120,768]{4,3,0,2,1:T(8,128)(2,1)} %bitcast.427), channel_id=1, source_target_pairs={{0,4},{4,0},{8,12},{12,8},{16,20},{20,16},{24,28},{28,24},{1,5},{5... | collective-permute-start | bytes 8847368 | tf_op jit(solution)/shard_map/ppermute | solution.py:130
  370.0 20.4 %collective-permute-start.27 = (bf16[512,768]{0,1:T(8,128)(2,1)}, bf16[512,768]{0,1:T(8,128)(2,1)}, u32[]{:S(2)}, u32[]{:S(2)}) collective-permute-start(bf16[512,768]{0,1:T(8,128)(2,1)} %convolution_convert_fusion.5), channel_id=1, source_target_pairs={{0,1},{4,5},{8,9},{12,13},{16,17},{20,21},{24,25},{28,29}} | collective-permute-start | bytes 2359304 | tf_op jit(solution)/shard_map/ppermute | solution.py:167
  375.4 21.6 %collective-permute-start.30 = (bf16[512,768]{0,1:T(8,128)(2,1)}, bf16[512,768]{0,1:T(8,128)(2,1)}, u32[]{:S(2)}, u32[]{:S(2)}) collective-permute-start(bf16[512,768]{0,1:T(8,128)(2,1)} %convolution_convert_fusion.4), channel_id=1, source_target_pairs={{3,2},{7,6},{11,10},{15,14},{19,18},{23,22},{27,26},{31,30}} | collective-permute-start | bytes 2359304 | tf_op jit(solution)/shard_map/ppermute | solution.py:168
  380.5 19.4 %collective-permute-start.33 = (bf16[1,2,2,96,576]{4,3,2,1,0:T(8,128)(2,1)S(1)}, bf16[1,2,2,96,576]{4,3,2,1,0:T(8,128)(2,1)S(1)}, u32[]{:S(2)}, u32[]{:S(2)}) collective-permute-start(bf16[1,2,2,96,576]{4,3,2,1,0:T(8,128)(2,1)S(1)} %slice_bitcast_fusion.16), channel_id=1, source_target_pairs={{0,4},{4,0},{8,12},{12,8},{16,20},{20,16},{24,28},{28,24},{1,5},{5... | collective-permute-start | bytes 1327112 | tf_op jit(solution)/shard_map/ppermute | solution.py:130
  392.5 20.9 %collective-permute-start.28 = (bf16[512,768]{0,1:T(8,128)(2,1)S(1)}, bf16[512,768]{0,1:T(8,128)(2,1)S(1)}, u32[]{:S(2)}, u32[]{:S(2)}) collective-permute-start(bf16[512,768]{0,1:T(8,128)(2,1)S(1)} %add_convert_fusion.3), channel_id=1, source_target_pairs={{0,1},{1,2},{4,5},{5,6},{8,9},{9,10},{12,13},{13,14},{16,17},{17,1... | collective-permute-start | bytes 2359304 | tf_op jit(solution)/shard_map/ppermute | solution.py:167
  399.0 19.8 %collective-permute-start.31 = (bf16[512,768]{0,1:T(8,128)(2,1)S(1)}, bf16[512,768]{0,1:T(8,128)(2,1)S(1)}, u32[]{:S(2)}, u32[]{:S(2)}) collective-permute-start(bf16[512,768]{0,1:T(8,128)(2,1)S(1)} %add_convert_fusion.1), channel_id=1, source_target_pairs={{3,2},{2,1},{7,6},{6,5},{11,10},{10,9},{15,14},{14,13},{19,18},{18... | collective-permute-start | bytes 2359304 | tf_op jit(solution)/shard_map/ppermute | solution.py:168
  400.1 28.7 %collective-permute-start.34 = (bf16[1,2,96,576]{3,2,1,0:T(8,128)(2,1)S(1)}, bf16[1,2,96,576]{3,2,1,0:T(8,128)(2,1)S(1)}, u32[]{:S(2)}, u32[]{:S(2)}) collective-permute-start(bf16[1,2,96,576]{3,2,1,0:T(8,128)(2,1)S(1)} %slice_bitcast_fusion.22), channel_id=1, source_target_pairs={{0,16},{4,20},{8,24},{12,28},{16,0},{20,4},{24,8},{28,12},{1,17},{... | collective-permute-start | bytes 663560 | tf_op jit(solution)/shard_map/ppermute | solution.py:130
  414.2 20.0 %collective-permute-start.29 = (bf16[512,768]{0,1:T(8,128)(2,1)S(1)}, bf16[512,768]{0,1:T(8,128)(2,1)S(1)}, u32[]{:S(2)}, u32[]{:S(2)}) collective-permute-start(bf16[512,768]{0,1:T(8,128)(2,1)S(1)} %add_convert_fusion.2), channel_id=1, source_target_pairs={{0,1},{1,2},{2,3},{4,5},{5,6},{6,7},{8,9},{9,10},{10,11},{12,13},{... | collective-permute-start | bytes 2359304 | tf_op jit(solution)/shard_map/ppermute | solution.py:167
  419.6 19.6 %collective-permute-start.32 = (bf16[512,768]{0,1:T(8,128)(2,1)S(1)}, bf16[512,768]{0,1:T(8,128)(2,1)S(1)}, u32[]{:S(2)}, u32[]{:S(2)}) collective-permute-start(bf16[512,768]{0,1:T(8,128)(2,1)S(1)} %add_convert_fusion), channel_id=1, source_target_pairs={{3,2},{2,1},{1,0},{7,6},{6,5},{5,4},{11,10},{10,9},{9,8},{15,14},{... | collective-permute-start | bytes 2359304 | tf_op jit(solution)/shard_map/ppermute | solution.py:168
  423.6 26.2 %collective-permute-start.43 = (bf16[4,2,96,768]{3,2,0,1:T(8,128)(2,1)S(1)}, bf16[4,2,96,768]{3,2,0,1:T(8,128)(2,1)S(1)}, u32[]{:S(2)}, u32[]{:S(2)}) collective-permute-start(bf16[4,2,96,768]{3,2,0,1:T(8,128)(2,1)S(1)} %slice_bitcast_fusion.4), channel_id=1, source_target_pairs={{0,8},{4,12},{8,0},{12,4},{16,24},{20,28},{24,16},{28,20},{1,9},{5... | collective-permute-start | bytes 3538952 | tf_op jit(solution)/shard_map/ppermute | solution.py:130
  427.4 35.3 %collective-permute-start.40 = (bf16[4,2,120,768]{3,2,0,1:T(8,128)(2,1)S(1)}, bf16[4,2,120,768]{3,2,0,1:T(8,128)(2,1)S(1)}, u32[]{:S(2)}, u32[]{:S(2)}) collective-permute-start(bf16[4,2,120,768]{3,2,0,1:T(8,128)(2,1)S(1)} %slice_bitcast_fusion.2), channel_id=1, source_target_pairs={{0,16},{4,20},{8,24},{12,28},{16,0},{20,4},{24,8},{28,12},{1,17},{... | collective-permute-start | bytes 4423688 | tf_op jit(solution)/shard_map/ppermute | solution.py:130
  450.2 22.3 %collective-permute-start.44 = (bf16[4,96,768]{2,1,0:T(8,128)(2,1)S(1)}, bf16[4,96,768]{2,1,0:T(8,128)(2,1)}, u32[]{:S(2)}, u32[]{:S(2)}) collective-permute-start(bf16[4,96,768]{2,1,0:T(8,128)(2,1)S(1)} %slice_bitcast_fusion.11), channel_id=1, source_target_pairs={{0,16},{4,20},{8,24},{12,28},{16,0},{20,4},{24,8},{28,12},{1,17},{... | collective-permute-start | bytes 1769480 | tf_op jit(solution)/shard_map/ppermute | solution.py:130
  466.6 17.8 %collective-permute-start.35 = (bf16[1,96,576]{2,1,0:T(8,128)(2,1)S(1)}, bf16[1,96,576]{2,1,0:T(8,128)(2,1)S(1)}, u32[]{:S(2)}, u32[]{:S(2)}) collective-permute-start(bf16[1,96,576]{2,1,0:T(8,128)(2,1)S(1)} %slice_bitcast_fusion.27), channel_id=1, source_target_pairs={{0,8},{4,12},{8,0},{12,4},{16,24},{20,28},{24,16},{28,20},{1,9},{5... | collective-permute-start | bytes 331784 | tf_op jit(solution)/shard_map/ppermute | solution.py:130
  467.8 17.6 %collective-permute-start.37 = (f32[1920]{0:T(1024)S(1)}, f32[1920]{0:T(1024)S(1)}, u32[]{:S(2)}, u32[]{:S(2)}) collective-permute-start(f32[1920]{0:T(1024)S(1)} %add.582), channel_id=1, source_target_pairs={{0,8},{4,12},{8,0},{12,4},{16,24},{20,28},{24,16},{28,20},{1,9},{5... | collective-permute-start | bytes 23048 | tf_op jit(solution)/shard_map/ppermute | solution.py:130
  496.7 23.1 %collective-permute-start.57 = (f32[1536]{0:T(1024)S(1)}, f32[1536]{0:T(1024)S(1)}, u32[]{:S(2)}, u32[]{:S(2)}) collective-permute-start(f32[1536]{0:T(1024)S(1)} %slice_add_fusion), channel_id=1, source_target_pairs={{0,2},{1,3},{2,0},{3,1},{4,6},{5,7},{6,4},{7,5},{8,10},{9,11},{10,... | collective-permute-start | bytes 18440 | tf_op jit(solution)/shard_map/ppermute | solution.py:130
  (110 other events, 1522.5 us)

commit v2 on v1

v2 whole, which is shorter than its diff:
```python
from functools import partial

import jax
import jax.numpy as jnp
from jax import lax
from jax.experimental import pallas as pl
from jax.experimental.pallas import tpu as pltpu
from jax.sharding import PartitionSpec as P

HEAD_DIM = 64
EPSILON = 1e-05
MASKED = -1000000000.0
BF = jnp.bfloat16
F32 = jnp.float32


def norm_parts(row_vals):
    row_mean = jnp.mean(row_vals, axis=-1, keepdims=True)
    centred = row_vals - row_mean
    inverse = lax.rsqrt(jnp.mean(centred * centred, axis=-1, keepdims=True) + EPSILON)
    return (centred * inverse, inverse)


def norm_back(grad_normed, normed, inverse):
    first_mean = jnp.mean(grad_normed, axis=-1, keepdims=True)
    second_mean = jnp.mean(grad_normed * normed, axis=-1, keepdims=True)
    return inverse * (grad_normed - first_mean - normed * second_mean)


def first_allowed(pack_lengths, pack_len):
    seq_ends = jnp.cumsum(pack_lengths, dtype=jnp.int32)
    seq_starts = seq_ends - pack_lengths
    places = jnp.arange(pack_len, dtype=jnp.int32)[None, :]
    inside = (places >= seq_starts[:, None]) & (places < seq_ends[:, None])
    started = jnp.max(jnp.where(inside, seq_starts[:, None], -1), axis=0, keepdims=True)
    return jnp.where(started >= 0, started, places)


def contract(left, right, left_dim, right_dim):
    return lax.dot_general(
        left, right, (((left_dim,), (right_dim,)), ((), ())), preferred_element_type=F32
    )


def join(parts):
    return parts[0] if len(parts) == 1 else jnp.concatenate(parts, axis=0)


def masked(scores, first, row):
    keys, queries = scores.shape
    parts = []
    if row:
        key_pos = lax.broadcasted_iota(jnp.int32, (row, queries), 0)
        parts.append(jnp.where(key_pos >= first, scores[:row], MASKED))
    key_pos = row + lax.broadcasted_iota(jnp.int32, (keys - row, queries), 0)
    query_pos = row + lax.broadcasted_iota(jnp.int32, (1, queries), 1)
    ok = (key_pos >= first) & (key_pos <= query_pos)
    parts.append(jnp.where(ok, scores[row:], MASKED))
    return parts


def query_block(rows):
    return min(256, rows)


def relative_block(place_ref, block, blocks):
    return lax.rem(block - place_ref[0] + blocks, blocks)


def forward_kernel(place_ref, qkv_ref, first_ref, att_ref, lse_ref, values_ref):
    blocks, each_rows = att_ref.shape[:2]
    rows = blocks * each_rows
    each = 3 * HEAD_DIM
    heads = qkv_ref.shape[1] // each
    block = query_block(each_rows)
    scale = jnp.asarray(HEAD_DIM**-0.5, BF)
    for row in range(0, rows, block):
        vals = [
            qkv_ref[row : row + block, (h + 1) * each - HEAD_DIM : (h + 1) * each]
            for h in range(heads)
        ]
        values_ref[:, row : row + block] = jnp.concatenate(vals, axis=1).astype(F32).T.astype(BF)
    for row in range(0, rows, block):
        end = row + block
        first = first_ref[:, row:end]
        outs = []
        for h in range(heads):
            c = h * each
            queries = qkv_ref[row:end, c : c + HEAD_DIM] * scale
            keys = qkv_ref[:end, c + HEAD_DIM : c + 2 * HEAD_DIM]
            scores = masked(contract(keys, queries, 1, 1), first, row)
            peak = jnp.max(scores[-1], axis=0, keepdims=True)
            if row:
                peak = jnp.maximum(peak, jnp.max(scores[0], axis=0, keepdims=True))
            exponents = [jnp.exp(part - peak) for part in scores]
            sums = sum(jnp.sum(part, axis=0, keepdims=True) for part in exponents)
            values = values_ref[h * HEAD_DIM : (h + 1) * HEAD_DIM, :end]
            low = join([part.astype(BF) for part in exponents])
            outs.append(contract(values, low, 1, 0) / sums)
            lse_ref[h : h + 1, row:end] = peak + jnp.log(sums)
        d = relative_block(place_ref, row // each_rows, blocks)
        at = row % each_rows
        att_ref[d, at : at + block, :] = jnp.concatenate(outs, axis=0).T.astype(BF)


def backward_kernel(head, place_ref, qkv_ref, att_ref, lse_ref, first_ref, *refs):
    grads_in, (out_ref, keys_ref, sum_ref, grad_ref) = refs[:-4], refs[-4:]
    blocks, each_rows = att_ref.shape[:2]
    rows = blocks * each_rows
    block = query_block(each_rows)
    scale = jnp.asarray(HEAD_DIM**-0.5, BF)
    c = head * 3 * HEAD_DIM
    e = head * HEAD_DIM
    for d, block_ref in enumerate(grads_in):
        grad_ref[d] = block_ref[:, e : e + HEAD_DIM]
    for row in range(0, rows, block):
        keys = qkv_ref[row : row + block, c + HEAD_DIM : c + 2 * HEAD_DIM] * scale
        keys_ref[:, row : row + block] = keys.astype(F32).T.astype(BF)
    sum_ref[...] = jnp.zeros_like(sum_ref)
    zero = jnp.zeros((block, HEAD_DIM), BF)
    for row in range(rows - block, -1, -block):
        end = row + block
        d = relative_block(place_ref, row // each_rows, blocks)
        at = row % each_rows
        queries = qkv_ref[row:end, c : c + HEAD_DIM] * scale
        keys = qkv_ref[:end, c + HEAD_DIM : c + 2 * HEAD_DIM]
        values = qkv_ref[:end, c + 2 * HEAD_DIM : c + 3 * HEAD_DIM]
        grad = grad_ref[d, at : at + block, :]
        att = att_ref[d, at : at + block, e : e + HEAD_DIM]
        delta = jnp.sum((grad.astype(F32) * att.astype(F32)).T, axis=0, keepdims=True)
        scores = masked(contract(keys, queries, 1, 1), first_ref[:, row:end], row)
        lse = lse_ref[head : head + 1, row:end]
        probs = join([jnp.exp(part - lse) for part in scores])
        grad_scores = (probs * (contract(values, grad, 1, 1) - delta)).astype(BF)
        grad_queries = contract(keys_ref[:, :end], grad_scores, 1, 0)
        out_ref[row:end, :HEAD_DIM] = grad_queries.T.astype(BF)
        right = jnp.concatenate(
            [
                jnp.concatenate([queries, zero], axis=1),
                jnp.concatenate([zero, grad], axis=1),
            ],
            axis=0,
        )
        left = jnp.concatenate([grad_scores, probs.astype(BF)], axis=1)
        sum_ref[:end, :] += jnp.dot(left, right, preferred_element_type=F32)
    out_ref[:, HEAD_DIM:] = sum_ref[...].astype(BF)


def kernel_call(kernel, out_shape, scratch_shapes, flops, place, *args):
    whole = pl.BlockSpec(memory_space=pltpu.VMEM)
    return pl.pallas_call(
        kernel,
        out_shape=out_shape,
        in_specs=[pl.BlockSpec(memory_space=pltpu.SMEM)] + [whole] * len(args),
        out_specs=jax.tree.map(lambda _: whole, out_shape),
        scratch_shapes=scratch_shapes,
        compiler_params=pltpu.CompilerParams(vmem_limit_bytes=48 * 2**20),
        cost_estimate=pl.CostEstimate(
            flops=flops, bytes_accessed=sum(a.size * 2 for a in args), transcendentals=flops // 64
        ),
    )(place, *args)


def attend_forward(place, qkv, first, blocks):
    rows, width = qkv.shape
    shapes = (
        jax.ShapeDtypeStruct((blocks, rows // blocks, width // 3), BF),
        jax.ShapeDtypeStruct((8 * pl.cdiv(width // (3 * HEAD_DIM), 8), rows), F32),
    )
    scratch = [pltpu.VMEM((width // 3, rows), BF)]
    flops = 8 * rows * rows * width // 3
    return kernel_call(forward_kernel, shapes, scratch, flops, place, qkv, first)


def attend_backward(head, place, qkv, att, lse, first, grads):
    blocks, each_rows = att.shape[:2]
    rows = qkv.shape[0]
    shape = jax.ShapeDtypeStruct((rows, 3 * HEAD_DIM), BF)
    scratch = [
        pltpu.VMEM((HEAD_DIM, rows), BF),
        pltpu.VMEM((rows, 2 * HEAD_DIM), F32),
        pltpu.VMEM((blocks, each_rows, HEAD_DIM), BF),
    ]
    flops = 2 * rows * rows * HEAD_DIM
    kernel = partial(backward_kernel, head)
    return kernel_call(kernel, shape, scratch, flops, place, qkv, att, lse, first, *grads)


def dp_bits():
    return (lax.axis_size("dp") - 1).bit_length()


def doubles():
    size = lax.axis_size("dp")
    return size == 1 << dp_bits() and 1 < size <= 8


def relative_blocks():
    size = lax.axis_size("dp")
    pos = jnp.arange(size, dtype=jnp.int32)
    if not doubles():
        return pos
    high = dp_bits() - 1
    return ((pos & ((1 << high) - 1)) << 1 | pos >> high) ^ lax.axis_index("dp")


def chosen_columns(width):
    each = width // lax.axis_size("dp")
    source = (relative_blocks()[:, None] * each + jnp.arange(each, dtype=jnp.int32)).reshape(-1)
    return (jnp.arange(width, dtype=jnp.int32)[:, None] == source[None, :]).astype(BF)


def flip(value, axis, bit):
    size = lax.axis_size(axis)
    return lax.ppermute(value, axis, [(i, i ^ (1 << bit)) for i in range(size)])


def after(value, other):
    return lax.optimization_barrier((value, other))[0]


def exchange(blocks):
    size = lax.axis_size("tensor")
    came = [
        lax.ppermute(blocks[d], "tensor", [(i, (i + d) % size) for i in range(size)])
        for d in range(1, size)
    ]
    return [blocks[0]] + came[::-1]


def fold(rows, width):
    groups = width // rows.shape[-1]
    each = rows.shape[-2] // groups
    return jnp.concatenate(
        [rows[..., g * each : (g + 1) * each, :] for g in range(groups)], axis=-1
    )


def unfold(rows, width):
    groups = rows.shape[-1] // width
    return jnp.concatenate([rows[..., g * width : (g + 1) * width] for g in range(groups)], axis=-2)


class Doubling:
    def __init__(self, block, upward):
        high = list(range(1, dp_bits()))
        self.block, self.shape, self.held, self.came = block, block.shape, [], None
        self.bits = (high if upward else high[::-1]) + [0] if doubles() else []

    def start(self):
        self.came = flip(self.block, "dp", self.bits[0]) if self.bits else self.block

    def step(self):
        if self.bits:
            bit = self.bits.pop(0)
            at = 1 + sum(b > bit for b in self.held) if bit else 1
            came = flip(self.block, "dp", bit) if self.came is None else self.came
            self.came = None
            self.block = jnp.stack([self.block, came], axis=at)
            self.held.append(bit)

    def result(self):
        while self.bits:
            self.step()
        if not self.held:
            return lax.all_gather(self.block, "dp", axis=1)
        return self.block.reshape(self.shape[0], lax.axis_size("dp"), *self.shape[1:])


class Halving:
    def __init__(self, parts, upward):
        bits = dp_bits()
        high = list(range(1, bits))
        self.block, self.bits, self.axes = parts, [], None
        if doubles():
            self.block = parts.reshape(parts.shape[0], *[2] * bits, *parts.shape[2:])
            self.bits = [0] + (high[::-1] if upward else high)
            self.axes = {0: 1, **{b: 1 + bits - b for b in high}}

    def step(self):
        if self.bits:
            bit = self.bits.pop(0)
            at = self.axes[bit]
            keep = lax.index_in_dim(self.block, 0, at, keepdims=False)
            came = flip(lax.index_in_dim(self.block, 1, at, keepdims=False), "dp", bit)
            self.block = (keep.astype(F32) + came.astype(F32)).astype(BF)
            self.axes = {b: a - (a > at) for b, a in self.axes.items()}

    def result(self):
        if self.axes is None:
            return lax.psum_scatter(self.block, "dp", scatter_dimension=1)
        while self.bits:
            self.step()
        return self.block


def total(vector, axis):
    for bit in range((lax.axis_size(axis) - 1).bit_length()):
        vector = vector + flip(vector, axis, bit)
    return vector


def on_device(
    inputs,
    lengths,
    w_qkv,
    b_qv,
    w_out,
    b_out,
    w_fc,
    b_fc,
    w_proj,
    b_proj,
    gain_one,
    shift_one,
    gain_two,
    shift_two,
    cotangent,
):
    row_count, model_width = inputs.shape[1:]
    tensor_size = lax.axis_size("tensor")
    dp_size = lax.axis_size("dp")
    tensor_pos = lax.axis_index("tensor")
    pack_len = row_count * tensor_size
    head_width = w_qkv.shape[2]
    local_heads = head_width // HEAD_DIM
    fc_local = b_fc.shape[0]
    owned = model_width // dp_size
    out_rows = owned * head_width // fc_local
    place = chosen_columns(model_width)

    def relative(rows):
        return jnp.dot(rows, place, preferred_element_type=F32)

    def absolute(rows):
        return jnp.einsum(
            "td,cd->tc",
            rows,
            place.astype(rows.dtype),
            precision=lax.Precision.HIGHEST,
            preferred_element_type=F32,
        )

    qkv_rows = w_qkv.reshape(3, owned, local_heads, HEAD_DIM).transpose(1, 2, 0, 3)
    qkv_full = Doubling(qkv_rows.reshape(1, owned, 3 * head_width), True).result()
    vectors = relative(jnp.stack([gain_one, shift_one, gain_two, shift_two, b_out, b_proj]))
    gain_first, shift_first, gain_second, shift_second, bias_out, bias_proj = vectors
    rows_in = relative(inputs[0])
    normed_one, _ = norm_parts(rows_in)
    h_one = (normed_one * gain_first + shift_first).astype(BF)
    h_one_all = lax.all_gather(h_one, "tensor", axis=0, tiled=True)

    shard = jnp.concatenate([w_fc, w_proj.T, fold(w_out.T, fc_local), b_fc[None]])
    shards = exchange([shard] * tensor_size)
    shards, qkv_full = lax.optimization_barrier((shards, qkv_full))
    qkv_full = qkv_full.reshape(model_width, 3 * head_width)

    bias_fc = jnp.stack([part[-1:] for part in shards]).astype(F32)
    outs = [unfold(part[2 * owned : -1], head_width) for part in shards]
    gathers = [
        Doubling(jnp.stack([part[:owned] for part in shards]), True),
        Doubling(jnp.stack([part[owned : 2 * owned] for part in shards]), False),
        Doubling(jnp.concatenate(outs, axis=1)[None], True),
    ]
    for gather in gathers:
        gather.step()
    held = lax.optimization_barrier([g.block for g in gathers])
    for gather, block in zip(gathers, held):
        gather.block = block

    place_on_line = tensor_pos.astype(jnp.int32).reshape(1)
    first = first_allowed(lengths[0, 0], pack_len)
    none = jnp.zeros_like(b_qv[0])
    bias_qkv = jnp.stack([b_qv[0], none, b_qv[1]]).astype(F32)
    bias_qkv = bias_qkv.reshape(3, local_heads, HEAD_DIM).transpose(1, 0, 2).reshape(-1)
    projected = jnp.dot(h_one_all, qkv_full, preferred_element_type=F32)
    qkv = (projected + bias_qkv).astype(BF)
    att_all, lse = attend_forward(place_on_line, qkv, first, tensor_size)
    for gather in gathers:
        gather.start()
    att_all, held = lax.optimization_barrier((att_all, [g.came for g in gathers]))
    for gather, came in zip(gathers, held):
        gather.came = came
        gather.step()
    att = exchange([att_all[d] for d in range(tensor_size)])
    att, held = lax.optimization_barrier((att, [g.block for g in gathers]))
    for gather, block in zip(gathers, held):
        gather.block = block
    att_rows = jnp.concatenate(att, axis=1)
    fc_full, proj_t, out_t = [gather.result() for gather in gathers]
    fc_full = fc_full.reshape(tensor_size, model_width, fc_local)
    proj_t = proj_t.reshape(tensor_size, model_width, fc_local)
    out_t = out_t.reshape(model_width, model_width)

    middle = (
        rows_in + jnp.einsum("tc,dc->td", att_rows, out_t, preferred_element_type=F32) + bias_out
    )
    normed_two, inverse_two = norm_parts(middle)
    h_two = (normed_two * gain_second + shift_second).astype(BF)
    pre_act = jnp.einsum("td,zdf->ztf", h_two, fc_full, preferred_element_type=F32) + bias_fc
    root = (2.0 / jnp.pi) ** 0.5
    bend = jnp.tanh(root * (pre_act + 0.044715 * pre_act * pre_act * pre_act))
    active = (0.5 * pre_act * (1.0 + bend)).astype(BF)
    slope = 0.5 * (1.0 + bend) + 0.5 * pre_act * (1.0 - bend * bend) * root * (
        1.0 + 3 * 0.044715 * pre_act * pre_act
    )
    grad_y = relative(cotangent[0])
    grad_low = grad_y.astype(BF)
    grad_active = jnp.einsum("td,zdf->ztf", grad_low, proj_t, preferred_element_type=F32)
    grad_pre = (grad_active * slope).astype(BF)
    grad_h_two = jnp.einsum("ztf,zdf->td", grad_pre, fc_full, preferred_element_type=F32)
    grad_middle = grad_y + norm_back(grad_h_two * gain_second, normed_two, inverse_two)
    grad_branch = grad_middle.astype(BF)
    grad_att_rows = jnp.dot(grad_branch, out_t, preferred_element_type=F32).astype(BF)
    grad_att = exchange(
        [grad_att_rows[:, d * head_width : (d + 1) * head_width] for d in range(tensor_size)]
    )


    def by_owner(left, right):
        full = jnp.einsum("td,ztf->zdf", left, right, preferred_element_type=F32).astype(BF)
        return full.reshape(tensor_size, dp_size, owned, fc_local)

    d_out_all = jnp.einsum(
        "td,tc->dc", grad_branch, att_rows, preferred_element_type=F32
    )
    parts = [
        Halving(by_owner(h_two, grad_pre), True),
        Halving(by_owner(grad_low, active), False),
        Halving(d_out_all.astype(BF).reshape(1, dp_size, owned, model_width), True),
    ]
    for part in parts:
        part.step()

    early_rows = jnp.stack(
        [
            jnp.sum(grad_h_two * normed_two, axis=0),
            jnp.sum(grad_h_two, axis=0),
            jnp.sum(grad_middle, axis=0),
            jnp.sum(grad_y, axis=0),
        ]
    )
    sums_fc = jnp.sum(grad_pre, axis=1, dtype=F32)

    by_head = []
    for head in range(local_heads):
        by_head.append(attend_backward(head, place_on_line, qkv, att_all, lse, first, grad_att))
        if head == 0:
            grad_att, held, by_head[0] = lax.optimization_barrier(
                (grad_att, [part.block for part in parts], by_head[0])
            )
            for part, block in zip(parts, held):
                part.block = block
                part.step()
    stacked = jnp.concatenate(by_head, axis=1)

    def tied(values):
        values, held = lax.optimization_barrier((values, [part.block for part in parts]))
        for part, block in zip(parts, held):
            part.block = block
        return values

    qkv_absolute = jnp.dot(place, qkv_full, preferred_element_type=F32).astype(BF)
    grad_middle = absolute(grad_middle)
    terms = jnp.einsum("te,ce->tc", stacked, qkv_absolute, preferred_element_type=F32).astype(BF)
    grad_h_one = lax.psum_scatter(terms, "tensor", scatter_dimension=0, tiled=True).astype(F32)
    stacked, grad_middle, terms = tied((stacked, grad_middle, terms))
    for part in parts:
        part.step()
    stacked = tied(stacked)
    mlp_out = jnp.einsum("ztf,zdf->td", after(active, terms), proj_t, preferred_element_type=F32)
    output = absolute((middle + mlp_out + bias_proj).astype(BF)).astype(BF)

    sums_fc_w, sums_proj_w, sums_out_w = [part.result() for part in parts]
    pieces = [
        jnp.concatenate(
            [
                sums_fc_w[d],
                sums_proj_w[d],
                fold(sums_out_w[0, :, d * head_width : (d + 1) * head_width], fc_local),
            ]
        )
        for d in range(tensor_size)
    ]
    pieces = exchange(pieces)
    d_shard = sum(came.astype(F32) for came in pieces)
    d_fc = d_shard[:owned]
    d_proj = d_shard[owned : 2 * owned].T
    d_out = unfold(d_shard[2 * owned :], head_width).T

    sums = jnp.sum(stacked, axis=0, dtype=F32)
    sums_by = sums.reshape(local_heads, 3, HEAD_DIM).transpose(1, 0, 2).reshape(3, head_width)
    sum_qv = sums_by[0::2]
    qkv_all = jnp.einsum(
        "td,te->de",
        h_one_all,
        stacked,
        preferred_element_type=F32,
    )
    wide_weights = qkv_full.astype(F32)
    normed_sums = (qkv_all - shift_first[:, None] * sums[None, :]) / gain_first[:, None]
    late_rows = jnp.stack(
        [
            jnp.sum(wide_weights * normed_sums, axis=1),
            jnp.sum(wide_weights * sums[None, :], axis=1),
        ]
    )
    d_qkv = Halving(qkv_all.astype(BF).reshape(1, dp_size, owned, 3 * head_width), True)
    d_qkv = d_qkv.result()[0]
    d_qkv = d_qkv.astype(F32).reshape(owned, local_heads, 3, HEAD_DIM).transpose(2, 0, 1, 3)
    d_qkv = d_qkv.reshape(3, owned, head_width)

    normed_rows, inverse_rows = norm_parts(inputs[0].astype(F32))
    grad_in = grad_middle + norm_back(
        grad_h_one * gain_one.astype(F32), normed_rows, inverse_rows
    )
    wide = model_width
    placed_fc = lax.dynamic_update_slice(
        jnp.zeros((2 * tensor_size, fc_local), F32), sums_fc, (tensor_pos, 0)
    )
    placed_fc = placed_fc[:tensor_size] + placed_fc[tensor_size:]
    rows = absolute(jnp.concatenate([early_rows, late_rows])).reshape(-1)
    sums_all = total(
        jnp.concatenate([rows, placed_fc.reshape(-1), sum_qv.reshape(-1)]), "dp"
    )
    sum_qv = sums_all[rows.size + placed_fc.size :].reshape(2, head_width)
    sums_all = after(sums_all[: rows.size + placed_fc.size], pieces)
    sums_all = total(sums_all, "tensor")
    d_gain_two, d_shift_two, d_b_out, d_b_proj, d_gain_one, d_shift_one = (
        sums_all[: 6 * wide].reshape(6, wide)
    )
    d_b_fc = lax.dynamic_slice(sums_all[6 * wide :], (tensor_pos * fc_local,), (fc_local,))
    return (
        output[None],
        grad_in[None],
        d_qkv,
        sum_qv,
        d_out,
        d_b_out,
        d_fc,
        d_b_fc,
        d_proj,
        d_b_proj,
        d_gain_one,
        d_shift_one,
        d_gain_two,
        d_shift_two,
    )


def solution(mesh):
    rows = P(None, ("dp", "tensor"), None)
    placed = (
        rows,
        P("dp", None, None),
        P(None, "dp", "tensor"),
        P(None, "tensor"),
        P("tensor", "dp"),
        P(),
        P("dp", "tensor"),
        P("tensor"),
        P("tensor", "dp"),
        P(),
        P(),
        P(),
        P(),
        P(),
        rows,
    )
    return jax.shard_map(
        on_device,
        mesh=mesh,
        in_specs=placed,
        out_specs=(
            rows,
            rows,
            P(None, "dp", "tensor"),
            P(None, "tensor"),
            P("tensor", "dp"),
            P(),
            P("dp", "tensor"),
            P("tensor"),
            P("tensor", "dp"),
            P(),
            P(),
            P(),
            P(),
            P(),
        ),
        check_vma=False,
    )
```

time: 534 us -> 411 us (0.77)
  matrix products: 126 us -> 62.5 us
  local copies, waits for them, and re-layouts: 86.2 us -> 42.7 us
  starting transfers between devices: 93.9 us -> 51.1 us
  Pallas kernels: 0 us -> 40.7 us
  other arithmetic: 82.6 us -> 54.1 us
  between operations: 3.25 us -> 15.8 us
  waiting for transfers between devices: 132 us -> 138 us
    dot_general x34 -> x5, matrix products: 76.2 us -> 14.2 us  [the longest x1 7.16 us: on_device(): jnp.einsum('te,ce->tc', stacked, qkv_absolute, preferred_element_type=F32)]
    ppermute x30 -> x12, starting transfers between devices: 66.2 us -> 25.5 us  [exchange(): lax.ppermute(blocks[d], 'tensor', [(i, (i + d) % size) for i in range(siz...]
    pallas_call x0 -> x4, Pallas kernels: none -> 40.7 us  [kernel_call(): pl.pallas_call(kernel, out_shape=out_shape, in_specs=[pl.BlockSpec(memory...]
    ppermute x30 -> x12, waiting for transfers between devices: 69.9 us -> 96 us  [exchange(): lax.ppermute(blocks[d], 'tensor', [(i, (i + d) % size) for i in range(siz...]
    unnamed x190, local copies, waits for them, and re-layouts: 28.8 us -> 8.92 us
    ppermute x28 -> x29, waiting for transfers between devices: 61.9 us -> 42 us  [flip(): return lax.ppermute(value, axis, [(i, i ^ 1 << bit) for i in range(size)])]
    convert_element_type x16 -> x13, other arithmetic: 27 us -> 13.5 us  [the longest x11 13.5 us: step(): self.block = (keep.astype(F32) + came.astype(F32)).astype(BF)]
    dynamic_slice x5 -> x1, local copies, waits for them, and re-layouts: 9.85 us -> 0.67 us  [on_device(): lax.dynamic_slice(sums_all[6 * wide:], (tensor_pos * fc_local,), (fc_loca...]
  transfers between devices with their start and end apart: 58 -> 43, of which waited for: 21 -> 19; matrix products, arithmetic and copies ran while one was open for 43% -> 26% of each run, Pallas kernels for 0% -> 10%
where the time goes in v2:
time: 411 us; the launch traced here: 405 us
  waiting for transfers between devices  138 us (34%)
  matrix products  62.5 us (15%)
  other arithmetic  54.1 us (13%)
  starting transfers between devices  51.1 us (12%)
  local copies, waits for them, and re-layouts  42.7 us (10%)
  Pallas kernels  40.7 us (10%)
  between operations  15.8 us (4%)
    ppermute x12, waiting for transfers between devices, exchange(): lax.ppermute(blocks[d], 'tensor', [(i, (i + d) % size) for i in range(siz...  96 us
    ppermute x29, waiting for transfers between devices, flip(): return lax.ppermute(value, axis, [(i, i ^ 1 << bit) for i in range(size)])  42 us
    pallas_call x4, Pallas kernels, kernel_call(): pl.pallas_call(kernel, out_shape=out_shape, in_specs=[pl.BlockSpec(memory...  40.7 us
    ppermute x29, starting transfers between devices, flip(): return lax.ppermute(value, axis, [(i, i ^ 1 << bit) for i in range(size)])  25.6 us
    ppermute x12, starting transfers between devices, exchange(): lax.ppermute(blocks[d], 'tensor', [(i, (i + d) % size) for i in range(siz...  25.5 us
    another operation x15, other arithmetic, step(): self.block = jnp.stack([self.block, came], axis=at)  23.1 us
    convert_element_type x11, other arithmetic, step(): self.block = (keep.astype(F32) + came.astype(F32)).astype(BF)  13.5 us
    dot_general x3, matrix products, absolute(): jnp.einsum('td,cd->tc', rows, place.astype(rows.dtype), precision=lax.Pre...  9.34 us
  transfers between devices with their start and end apart: 43, of which 19 were waited for; matrix products, arithmetic and copies ran while one was open for 26% of the time, Pallas kernels for 10%

profile of v2, /device:TPU:0, one launch (start us, length us, event | category | flops | bytes accessed | tf_op | source)
XLA Modules:
  0.0 405.1 jit_solution(17507886750534645019)
XLA Ops:
  12.6 3.0 collective-permute-start.3
  16.8 3.7 collective-permute-start
  23.4 6.0 %collective-permute-done.4 = bf16[1,2,96,576]{2,3,1,0:T(8,128)(2,1)S(1)} collective-permute-done((bf16[1,2,96,576]{2,3,1,0:T(8,128)(2,1)S(1)}, bf16[1,2,96,576]{2,3,1,0:T(8,128)(2,1)S(1)}, u32[]{:S(2)}, u32[]{:S(2)}) %collective-permute-start.4) | collective-permute-done | bytes 221216 | tf_op jit(solution)/shard_map/ppermute | solution.py:215
  34.3 41.1 %collective-permute-done.1 = bf16[217,768]{1,0:T(8,128)(2,1)} collective-permute-done((bf16[217,768]{1,0:T(8,128)(2,1)S(1)}, bf16[217,768]{1,0:T(8,128)(2,1)}, u32[]{:S(2)}, u32[]{:S(2)}) %collective-permute-start.1) | collective-permute-done | bytes 333344 | tf_op jit(solution)/shard_map/ppermute | solution.py:225
  89.3 7.4 %collective-permute-done.6 = bf16[4,96,768]{2,1,0:T(8,128)(2,1)} collective-permute-done((bf16[4,96,768]{2,1,0:T(8,128)(2,1)}, bf16[4,96,768]{2,1,0:T(8,128)(2,1)}, u32[]{:S(2)}, u32[]{:S(2)}) %collective-permute-start.6) | collective-permute-done | bytes 589856 | tf_op jit(solution)/shard_map/ppermute | solution.py:215
  103.2 4.6 %add_convert_fusion.qkv_ref = bf16[2048,576]{1,0:T(8,128)(2,1)S(1)} fusion(bf16[2048,768]{0,1:T(8,128)(2,1)} %all-gather.2.cloned.1.call-done, bf16[768,576]{1,0:T(8,128)(2,1)S(1)} %bitcast.324, f32[576]{0:T(1024)S(1)} %reshape.394), kind=kOutput, calls=%fused_computation.13 | convolution fusion | flops 1814298624 | bytes 6392064 | tf_op jit(solution)/shard_map/dot_general | solution.py:376
  107.8 19.1 %shard_map.254 = (bf16[4,512,192]{2,1,0:T(8,128)(2,1)S(1)}, f32[8,2048]{1,0:T(8,128)S(1)}) custom-call(s32[1]{0:T(128)} %bitcast.2.place_ref, bf16[2048,576]{1,0:T(8,128)(2,1)S(1)} %add_convert_fusion.qkv_ref, s32[1,2048]{1,0:T(1,128)S(1)} %compare_select_fusion.first_ref), custom_call_target="tpu_custom_call" | custom-call | flops 6442450944 | bytes 2363392 | tf_op jit(solution)/shard_map/pallas_call | solution.py:151
  128.5 12.2 %collective-permute-start.13 = (bf16[512,192]{1,0:T(8,128)(2,1)S(1)}, bf16[512,192]{1,0:T(8,128)(2,1)S(1)}, u32[]{:S(2)}, u32[]{:S(2)}) collective-permute-start(bf16[512,192]{1,0:T(8,128)(2,1)S(1)} %get-tuple-element.186), channel_id=1, source_target_pairs={{0,2},{1,3},{2,0},{3,1},{4,6},{5,7},{6,4},{7,5},{8,10},{9,11},{10,... | collective-permute-start | bytes 589832 | tf_op jit(solution)/shard_map/ppermute | solution.py:225
  142.8 2.9 pad_maximum_fusion.4
  146.8 3.3 pad_maximum_fusion.3
  150.1 7.9 %collective-permute-done.13 = bf16[512,192]{1,0:T(8,128)(2,1)S(1)} collective-permute-done((bf16[512,192]{1,0:T(8,128)(2,1)S(1)}, bf16[512,192]{1,0:T(8,128)(2,1)S(1)}, u32[]{:S(2)}, u32[]{:S(2)}) %collective-permute-start.13) | collective-permute-done | bytes 196640 | tf_op jit(solution)/shard_map/ppermute | solution.py:225
  161.0 3.1 copy.156
  173.9 2.8 pad_maximum_fusion.1
  177.1 4.5 %pad_maximum_fusion = bf16[4,2,2,2,96,768]{5,4,0,3,2,1:T(8,128)(2,1)S(1)} fusion(bf16[4,1,2,2,96,768]{5,4,0,3,2,1:T(8,128)(2,1)} %bitcast.51, bf16[4,1,2,2,96,768]{5,4,0,3,2,1:T(8,128)(2,1)} %bitcast.50), kind=kLoop, calls=%fused_computation.14 | loop fusion | flops 2359296 | bytes 9437184 | tf_op jit(solution)/shard_map/stack | solution.py:259
  182.3 4.6 %multiply_convert_fusion = (bf16[4,512,768]{2,1,0:T(8,128)(2,1)S(1)}, f32[4,768,512]{1,2,0:T(8,128)S(1)}) fusion(f32[4,768]{1,0:T(4,128)S(1)} %maximum_convert_fusion, bf16[4,768,768]{2,1,0:T(8,128)(2,1)S(1)} %bitcast.321, f32[512,768]{0,1:T(8,128)S(1)} %get-tuple-element.268, f32[768]{0:T(1024)S(1)} %copy-done.64, f32[768]{0:T(1024)S(1)} %copy-done.48, ...), kind=kOutput, calls=%fused_computation.11 | convolution fusion | flops 2433613824 | bytes 15751168 | tf_op jit(solution)/shard_map/td,zdf->ztf/dot_general | solution.py:400
  186.9 6.6 %convert_reduce_fusion = (f32[4,768]{1,0:T(4,128)S(1)}, bf16[4,512,768]{2,1,0:T(8,128)(2,1)S(1)}) fusion(f32[4,768,512]{1,2,0:T(8,128)S(1)} %get-tuple-element.270, f32[4,768]{1,0:T(4,128)S(1)} %maximum_convert_fusion, bf16[4,768,768]{2,1,0:T(8,128)(2,1)S(1)} %bitcast.311, f32[768,512]{1,0:T(8,128)S(1)} %copy-done.17), kind=kOutput, calls=%fused_computation.10 | convolution fusion | flops 2450912256 | bytes 15753216 | tf_op jit(solution)/shard_map/td,zdf->ztf/dot_general | solution.py:409
  193.6 4.4 %fusion.88 = (f32[768]{0:T(1024)}, f32[512,768]{1,0:T(8,128)}) fusion(bf16[4,512,768]{2,1,0:T(8,128)(2,1)S(1)} %get-tuple-element.277, bf16[4,768,768]{2,1,0:T(8,128)(2,1)S(1)} %bitcast.322), kind=kOutput, calls=%fused_computation.238 | convolution fusion | flops 2416311552 | bytes 9440256 | tf_op jit(solution)/shard_map/ztf,zdf->td/dot_general | solution.py:411
  197.9 4.9 %convolution_convert_fusion.2 = bf16[4,768,768]{1,2,0:T(8,128)(2,1)} fusion(bf16[4,512,768]{2,1,0:T(8,128)(2,1)S(1)} %get-tuple-element.277, f32[512,768]{0,1:T(8,128)S(1)} %get-tuple-element.268, f32[768]{0:T(1024)S(1)} %copy-done.64, f32[768]{0:T(1024)S(1)} %copy-done.48, f32[512]{0:T(512)S(1)} %add_rsqrt_fusion.1, f32[512]{0:T(512)S(1)} %broadcast_multiply_fusion.5), kind=kOutput, calls=%fused_computation.22 | convolution fusion | flops 2420244480 | bytes 9447424 | tf_op jit(solution)/shard_map/td,ztf->zdf/dot_general | solution.py:421
  202.8 4.3 %convolution_convert_fusion.1 = bf16[4,768,768]{1,2,0:T(8,128)(2,1)} fusion(bf16[4,512,768]{2,1,0:T(8,128)(2,1)S(1)} %get-tuple-element.269, f32[768,512]{1,0:T(8,128)S(1)} %copy-done.17), kind=kOutput, calls=%fused_computation.21 | convolution fusion | flops 2418671616 | bytes 9437184 | tf_op jit(solution)/shard_map/td,ztf->zdf/dot_general | solution.py:421
  207.1 3.0 copy.158
  226.2 3.5 fusion.29
  231.9 6.5 %fusion.13 = f32[512,768]{1,0:T(8,128)} fusion(f32[512,768]{0,1:T(8,128)} %copy-done.25, s32[768]{0:T(1024)S(1)} %copy-done.61), kind=kOutput, calls=%fused_computation.38 | convolution fusion | flops 3624468480 | bytes 3148800 | tf_op jit(solution)/shard_map/td,cd->tc/dot_general | solution.py:336
  238.4 2.9 collective-permute-done.20.refs_3_
  241.3 7.1 %shard_map.255 = bf16[2048,192]{1,0:T(8,128)(2,1)S(1)} custom-call(s32[1]{0:T(128)} %bitcast.2.place_ref, bf16[2048,576]{1,0:T(8,128)(2,1)S(1)} %copy-done.3, bf16[4,512,192]{2,1,0:T(8,128)(2,1)S(1)} %get-tuple-element.62.att_ref, f32[8,2048]{1,0:T(8,128)S(1)} %get-tuple-element.73.lse_ref, s32[1,2048]{1,0:T(1,128)S(1)} %compare_select_fusion.first_ref, ...), custom_call_target="tpu_custom_call" | custom-call | flops 536870912 | bytes 3969024 | tf_op jit(solution)/shard_map/pallas_call | solution.py:151
  252.3 3.3 fusion.8
  260.2 7.1 %shard_map.256 = bf16[2048,192]{1,0:T(8,128)(2,1)S(1)} custom-call(s32[1]{0:T(128)} %bitcast.2.place_ref, bf16[2048,576]{1,0:T(8,128)(2,1)S(1)} %copy-done.3, bf16[4,512,192]{2,1,0:T(8,128)(2,1)S(1)} %get-tuple-element.62.att_ref, f32[8,2048]{1,0:T(8,128)S(1)} %get-tuple-element.73.lse_ref, s32[1,2048]{1,0:T(1,128)S(1)} %compare_select_fusion.first_ref, ...), custom_call_target="tpu_custom_call" | custom-call | flops 536870912 | bytes 3969024 | tf_op jit(solution)/shard_map/pallas_call | solution.py:151
  267.3 7.5 %shard_map.257 = bf16[2048,192]{1,0:T(8,128)(2,1)S(1)} custom-call(s32[1]{0:T(128)} %bitcast.2.place_ref, bf16[2048,576]{1,0:T(8,128)(2,1)S(1)} %copy-done.3, bf16[4,512,192]{2,1,0:T(8,128)(2,1)S(1)} %get-tuple-element.62.att_ref, f32[8,2048]{1,0:T(8,128)S(1)} %get-tuple-element.73.lse_ref, s32[1,2048]{1,0:T(1,128)S(1)} %compare_select_fusion.first_ref, ...), custom_call_target="tpu_custom_call" | custom-call | flops 536870912 | bytes 3969024 | tf_op jit(solution)/shard_map/pallas_call | solution.py:151
  277.4 7.2 %convolution_convert_fusion = bf16[2048,768]{1,0:T(8,128)(2,1)} fusion(bf16[2048,576]{1,0:T(8,128)(2,1)} %pad_maximum_fusion.2, bf16[768,576]{1,0:T(8,128)(2,1)S(1)} %bitcast.326, s32[768]{0:T(1024)S(1)} %copy-done.61), kind=kOutput, calls=%fused_computation.20 | convolution fusion | flops 2494021632 | bytes 6392832 | tf_op jit(solution)/shard_map/te,ce->tc/dot_general | solution.py:465
  298.5 8.9 %collective-permute-done.28 = bf16[4,96,768]{2,1,0:T(8,128)(2,1)} collective-permute-done((bf16[4,96,768]{2,1,0:T(8,128)(2,1)}, bf16[4,96,768]{2,1,0:T(8,128)(2,1)}, u32[]{:S(2)}, u32[]{:S(2)}) %collective-permute-start.28) | collective-permute-done | bytes 589856 | tf_op jit(solution)/shard_map/ppermute | solution.py:215
  316.8 5.1 %multiply_reduce_fusion.1 = (f32[768]{0:T(1024)S(1)}, bf16[768,576]{0,1:T(8,128)(2,1)S(1)}) fusion(bf16[768,576]{0,1:T(8,128)(2,1)S(1)} %copy-done.33, f32[768]{0:T(1024)S(1)} %copy-done.52, f32[576]{0:T(1024)S(1)} %convert_reduce_fusion.1, f32[768]{0:T(1024)S(1)} %copy-done.50, bf16[2048,768]{0,1:T(8,128)(2,1)} %all-gather.2.cloned.1.call-done, ...), kind=kOutput, calls=%fused_computation.49 | convolution fusion | flops 1815035136 | bytes 7286016 | tf_op jit(solution)/shard_map/td,te->de/dot_general | solution.py:494
  329.9 3.2 collective-permute-done.35
  334.8 43.1 %collective-permute-done.37 = bf16[216,768]{1,0:T(8,128)(2,1)} collective-permute-done((bf16[216,768]{1,0:T(8,128)(2,1)}, bf16[216,768]{1,0:T(8,128)(2,1)}, u32[]{:S(2)}, u32[]{:S(2)}) %collective-permute-start.37) | collective-permute-done | bytes 331808 | tf_op jit(solution)/shard_map/ppermute | solution.py:225
  (420 shorter events, 134.6 us)
Async XLA Ops:
  7.2 96.0 %all-gather.2.cloned.1.call-start = ((), (), s32[]{:S(2)}) async-start(), calls=%async_computation.1 | async-start | bytes 3932160 | tf_op jit(solution)/shard_map/all_gather | solution.py:351
  12.4 382.1 %reduce-scatter.2.cloned.1.call-start = ((), (), s32[]{:S(2)}) async-start(), calls=%async_computation.2 | async-start | bytes 3932160 | tf_op jit(solution)/shard_map/reduce_scatter | solution.py:466
  12.6 9.0 %collective-permute-start.3 = (bf16[1,96,576]{1,2,0:T(8,128)(2,1)S(1)}, bf16[1,96,576]{1,2,0:T(8,128)(2,1)S(1)}, u32[]{:S(2)}, u32[]{:S(2)}) collective-permute-start(bf16[1,96,576]{1,2,0:T(8,128)(2,1)S(1)} %bitcast.338), channel_id=1, source_target_pairs={{0,8},{4,12},{8,0},{12,4},{16,24},{20,28},{24,16},{28,20},{1,9},{5... | collective-permute-start | bytes 331784 | tf_op jit(solution)/shard_map/ppermute | solution.py:215
  16.8 17.5 %collective-permute-start = (bf16[217,768]{1,0:T(8,128)(2,1)S(1)}, bf16[217,768]{1,0:T(8,128)(2,1)S(1)}, u32[]{:S(2)}, u32[]{:S(2)}) collective-permute-start(bf16[217,768]{1,0:T(8,128)(2,1)S(1)} %pad_maximum_fusion.14), channel_id=1, source_target_pairs={{0,3},{1,0},{2,1},{3,2},{4,7},{5,4},{6,5},{7,6},{8,11},{9,8},{10,9... | collective-permute-start | bytes 999944 | tf_op jit(solution)/shard_map/ppermute | solution.py:225
  20.4 55.0 %collective-permute-start.1 = (bf16[217,768]{1,0:T(8,128)(2,1)S(1)}, bf16[217,768]{1,0:T(8,128)(2,1)}, u32[]{:S(2)}, u32[]{:S(2)}) collective-permute-start(bf16[217,768]{1,0:T(8,128)(2,1)S(1)} %pad_maximum_fusion.14), channel_id=1, source_target_pairs={{0,2},{1,3},{2,0},{3,1},{4,6},{5,7},{6,4},{7,5},{8,10},{9,11},{10,... | collective-permute-start | bytes 999944 | tf_op jit(solution)/shard_map/ppermute | solution.py:225
  20.4 55.0 %collective-permute-start.2 = (bf16[217,768]{1,0:T(8,128)(2,1)S(1)}, bf16[217,768]{1,0:T(8,128)(2,1)}, u32[]{:S(2)}, u32[]{:S(2)}) collective-permute-start(bf16[217,768]{1,0:T(8,128)(2,1)S(1)} %pad_maximum_fusion.14), channel_id=1, source_target_pairs={{0,1},{1,2},{2,3},{3,0},{4,5},{5,6},{6,7},{7,4},{8,9},{9,10},{10,1... | collective-permute-start | bytes 999944 | tf_op jit(solution)/shard_map/ppermute | solution.py:225
  77.8 10.2 %collective-permute-start.7 = (bf16[4,96,768]{2,1,0:T(8,128)(2,1)}, bf16[4,96,768]{2,1,0:T(8,128)(2,1)}, u32[]{:S(2)}, u32[]{:S(2)}) collective-permute-start(bf16[4,96,768]{2,1,0:T(8,128)(2,1)} %get-tuple-element.208), channel_id=1, source_target_pairs={{0,16},{4,20},{8,24},{12,28},{16,0},{20,4},{24,8},{28,12},{1,17},{... | collective-permute-start | bytes 1769480 | tf_op jit(solution)/shard_map/ppermute | solution.py:215
  81.8 15.0 %collective-permute-start.6 = (bf16[4,96,768]{2,1,0:T(8,128)(2,1)}, bf16[4,96,768]{2,1,0:T(8,128)(2,1)}, u32[]{:S(2)}, u32[]{:S(2)}) collective-permute-start(bf16[4,96,768]{2,1,0:T(8,128)(2,1)} %get-tuple-element.210), channel_id=1, source_target_pairs={{0,8},{4,12},{8,0},{12,4},{16,24},{20,28},{24,16},{28,20},{1,9},{5... | collective-permute-start | bytes 1769480 | tf_op jit(solution)/shard_map/ppermute | solution.py:215
  99.1 27.8 %collective-permute-start.10 = (bf16[4,2,96,768]{3,2,0,1:T(8,128)(2,1)S(1)}, bf16[4,2,96,768]{3,2,0,1:T(8,128)(2,1)}, u32[]{:S(2)}, u32[]{:S(2)}) collective-permute-start(bf16[4,2,96,768]{3,2,0,1:T(8,128)(2,1)S(1)} %pad_maximum_fusion.7), channel_id=1, source_target_pairs={{0,8},{4,12},{8,0},{12,4},{16,24},{20,28},{24,16},{28,20},{1,9},{5... | collective-permute-start | bytes 3538952 | tf_op jit(solution)/shard_map/ppermute | solution.py:215
  101.1 25.7 %collective-permute-start.9 = (bf16[4,2,96,768]{3,2,0,1:T(8,128)(2,1)}, bf16[4,2,96,768]{3,2,0,1:T(8,128)(2,1)}, u32[]{:S(2)}, u32[]{:S(2)}) collective-permute-start(bf16[4,2,96,768]{3,2,0,1:T(8,128)(2,1)} %pad_maximum_fusion.6), channel_id=1, source_target_pairs={{0,16},{4,20},{8,24},{12,28},{16,0},{20,4},{24,8},{28,12},{1,17},{... | collective-permute-start | bytes 3538952 | tf_op jit(solution)/shard_map/ppermute | solution.py:215
  101.6 25.2 %collective-permute-start.11 = (bf16[1,2,96,768]{3,2,1,0:T(8,128)(2,1)S(1)}, bf16[1,2,96,768]{3,2,1,0:T(8,128)(2,1)}, u32[]{:S(2)}, u32[]{:S(2)}) collective-permute-start(bf16[1,2,96,768]{3,2,1,0:T(8,128)(2,1)S(1)} %pad_maximum_fusion.16), channel_id=1, source_target_pairs={{0,16},{4,20},{8,24},{12,28},{16,0},{20,4},{24,8},{28,12},{1,17},{... | collective-permute-start | bytes 884744 | tf_op jit(solution)/shard_map/ppermute | solution.py:215
  127.6 22.4 %collective-permute-start.12 = (bf16[512,192]{1,0:T(8,128)(2,1)S(1)}, bf16[512,192]{1,0:T(8,128)(2,1)S(1)}, u32[]{:S(2)}, u32[]{:S(2)}) collective-permute-start(bf16[512,192]{1,0:T(8,128)(2,1)S(1)} %get-tuple-element.187), channel_id=1, source_target_pairs={{0,3},{1,0},{2,1},{3,2},{4,7},{5,4},{6,5},{7,6},{8,11},{9,8},{10,9... | collective-permute-start | bytes 589832 | tf_op jit(solution)/shard_map/ppermute | solution.py:225
  128.5 29.5 %collective-permute-start.13 = (bf16[512,192]{1,0:T(8,128)(2,1)S(1)}, bf16[512,192]{1,0:T(8,128)(2,1)S(1)}, u32[]{:S(2)}, u32[]{:S(2)}) collective-permute-start(bf16[512,192]{1,0:T(8,128)(2,1)S(1)} %get-tuple-element.186), channel_id=1, source_target_pairs={{0,2},{1,3},{2,0},{3,1},{4,6},{5,7},{6,4},{7,5},{8,10},{9,11},{10,... | collective-permute-start | bytes 589832 | tf_op jit(solution)/shard_map/ppermute | solution.py:225
  140.8 17.2 %collective-permute-start.14 = (bf16[512,192]{1,0:T(8,128)(2,1)S(1)}, bf16[512,192]{1,0:T(8,128)(2,1)S(1)}, u32[]{:S(2)}, u32[]{:S(2)}) collective-permute-start(bf16[512,192]{1,0:T(8,128)(2,1)S(1)} %get-tuple-element.185), channel_id=1, source_target_pairs={{0,1},{1,2},{2,3},{3,0},{4,5},{5,6},{6,7},{7,4},{8,9},{9,10},{10,1... | collective-permute-start | bytes 589832 | tf_op jit(solution)/shard_map/ppermute | solution.py:225
  158.0 15.9 %collective-permute-start.17 = (bf16[4,2,2,96,768]{4,3,0,1,2:T(8,128)(2,1)}, bf16[4,2,2,96,768]{4,3,0,1,2:T(8,128)(2,1)}, u32[]{:S(2)}, u32[]{:S(2)}) collective-permute-start(bf16[4,2,2,96,768]{4,3,0,1,2:T(8,128)(2,1)} %pad_maximum_fusion.4), channel_id=1, source_target_pairs={{0,4},{4,0},{8,12},{12,8},{16,20},{20,16},{24,28},{28,24},{1,5},{5... | collective-permute-start | bytes 7077896 | tf_op jit(solution)/shard_map/ppermute | solution.py:215
  158.3 18.8 %collective-permute-start.16 = (bf16[4,2,2,96,768]{4,3,0,2,1:T(8,128)(2,1)}, bf16[4,2,2,96,768]{4,3,0,2,1:T(8,128)(2,1)}, u32[]{:S(2)}, u32[]{:S(2)}) collective-permute-start(bf16[4,2,2,96,768]{4,3,0,2,1:T(8,128)(2,1)} %pad_maximum_fusion.3), channel_id=1, source_target_pairs={{0,4},{4,0},{8,12},{12,8},{16,20},{20,16},{24,28},{28,24},{1,5},{5... | collective-permute-start | bytes 7077896 | tf_op jit(solution)/shard_map/ppermute | solution.py:215
  160.9 8.9 %collective-permute-start.15 = (bf16[1,2,2,96,768]{4,3,2,1,0:T(8,128)(2,1)S(1)}, bf16[1,2,2,96,768]{4,3,2,1,0:T(8,128)(2,1)S(1)}, u32[]{:S(2)}, u32[]{:S(2)}) collective-permute-start(bf16[1,2,2,96,768]{4,3,2,1,0:T(8,128)(2,1)S(1)} %pad_maximum_fusion.13), channel_id=1, source_target_pairs={{0,4},{4,0},{8,12},{12,8},{16,20},{20,16},{24,28},{28,24},{1,5},{5... | collective-permute-start | bytes 1769480 | tf_op jit(solution)/shard_map/ppermute | solution.py:215
  215.8 14.0 %collective-permute-start.18 = (bf16[512,192]{1,0:T(8,128)(2,1)}, bf16[512,192]{1,0:T(8,128)(2,1)S(1)}, u32[]{:S(2)}, u32[]{:S(2)}) collective-permute-start(bf16[512,192]{1,0:T(8,128)(2,1)} %get-tuple-element.191), channel_id=1, source_target_pairs={{0,3},{1,0},{2,1},{3,2},{4,7},{5,4},{6,5},{7,6},{8,11},{9,8},{10,9... | collective-permute-start | bytes 589832 | tf_op jit(solution)/shard_map/ppermute | solution.py:225
  215.8 22.5 %collective-permute-start.19 = (bf16[512,192]{1,0:T(8,128)(2,1)}, bf16[512,192]{1,0:T(8,128)(2,1)S(1)}, u32[]{:S(2)}, u32[]{:S(2)}) collective-permute-start(bf16[512,192]{1,0:T(8,128)(2,1)} %get-tuple-element.190), channel_id=1, source_target_pairs={{0,2},{1,3},{2,0},{3,1},{4,6},{5,7},{6,4},{7,5},{8,10},{9,11},{10,... | collective-permute-start | bytes 589832 | tf_op jit(solution)/shard_map/ppermute | solution.py:225
  219.2 30.5 %collective-permute-start.22 = (bf16[4,2,2,96,768]{4,3,0,1,2:T(8,128)(2,1)}, bf16[4,2,2,96,768]{4,3,0,1,2:T(8,128)(2,1)}, u32[]{:S(2)}, u32[]{:S(2)}) collective-permute-start(bf16[4,2,2,96,768]{4,3,0,1,2:T(8,128)(2,1)} %bitcast.306), channel_id=1, source_target_pairs={{0,4},{4,0},{8,12},{12,8},{16,20},{20,16},{24,28},{28,24},{1,5},{5... | collective-permute-start | bytes 7077896 | tf_op jit(solution)/shard_map/ppermute | solution.py:215
  223.1 29.2 %collective-permute-start.21 = (bf16[4,2,2,96,768]{4,3,0,2,1:T(8,128)(2,1)}, bf16[4,2,2,96,768]{4,3,0,2,1:T(8,128)(2,1)}, u32[]{:S(2)}, u32[]{:S(2)}) collective-permute-start(bf16[4,2,2,96,768]{4,3,0,2,1:T(8,128)(2,1)} %bitcast.307), channel_id=1, source_target_pairs={{0,4},{4,0},{8,12},{12,8},{16,20},{20,16},{24,28},{28,24},{1,5},{5... | collective-permute-start | bytes 7077896 | tf_op jit(solution)/shard_map/ppermute | solution.py:215
  225.7 22.7 %collective-permute-start.23 = (bf16[1,2,2,96,768]{4,3,2,1,0:T(8,128)(2,1)}, bf16[1,2,2,96,768]{4,3,2,1,0:T(8,128)(2,1)}, u32[]{:S(2)}, u32[]{:S(2)}) collective-permute-start(bf16[1,2,2,96,768]{4,3,2,1,0:T(8,128)(2,1)} %slice_bitcast_fusion.2), channel_id=1, source_target_pairs={{0,4},{4,0},{8,12},{12,8},{16,20},{20,16},{24,28},{28,24},{1,5},{5... | collective-permute-start | bytes 1769480 | tf_op jit(solution)/shard_map/ppermute | solution.py:215
  229.9 11.4 %collective-permute-start.20 = (bf16[512,192]{1,0:T(8,128)(2,1)}, bf16[512,192]{1,0:T(8,128)(2,1)S(1)}, u32[]{:S(2)}, u32[]{:S(2)}) collective-permute-start(bf16[512,192]{1,0:T(8,128)(2,1)} %get-tuple-element.189), channel_id=1, source_target_pairs={{0,1},{1,2},{2,3},{3,0},{4,5},{5,6},{6,7},{7,4},{8,9},{9,10},{10,1... | collective-permute-start | bytes 589832 | tf_op jit(solution)/shard_map/ppermute | solution.py:225
  255.9 28.6 %collective-permute-start.26 = (bf16[1,2,96,768]{3,2,1,0:T(8,128)(2,1)S(1)}, bf16[1,2,96,768]{3,2,1,0:T(8,128)(2,1)S(1)}, u32[]{:S(2)}, u32[]{:S(2)}) collective-permute-start(bf16[1,2,96,768]{3,2,1,0:T(8,128)(2,1)S(1)} %slice_bitcast_fusion.9), channel_id=1, source_target_pairs={{0,16},{4,20},{8,24},{12,28},{16,0},{20,4},{24,8},{28,12},{1,17},{... | collective-permute-start | bytes 884744 | tf_op jit(solution)/shard_map/ppermute | solution.py:215
  257.5 28.0 %collective-permute-start.25 = (bf16[4,2,96,768]{3,2,0,1:T(8,128)(2,1)}, bf16[4,2,96,768]{3,2,0,1:T(8,128)(2,1)}, u32[]{:S(2)}, u32[]{:S(2)}) collective-permute-start(bf16[4,2,96,768]{3,2,0,1:T(8,128)(2,1)} %slice_bitcast_fusion), channel_id=1, source_target_pairs={{0,8},{4,12},{8,0},{12,4},{16,24},{20,28},{24,16},{28,20},{1,9},{5... | collective-permute-start | bytes 3538952 | tf_op jit(solution)/shard_map/ppermute | solution.py:215
  258.6 31.6 %collective-permute-start.24 = (bf16[4,2,96,768]{3,2,0,1:T(8,128)(2,1)}, bf16[4,2,96,768]{3,2,0,1:T(8,128)(2,1)}, u32[]{:S(2)}, u32[]{:S(2)}) collective-permute-start(bf16[4,2,96,768]{3,2,0,1:T(8,128)(2,1)} %slice_bitcast_fusion.1), channel_id=1, source_target_pairs={{0,16},{4,20},{8,24},{12,28},{16,0},{20,4},{24,8},{28,12},{1,17},{... | collective-permute-start | bytes 3538952 | tf_op jit(solution)/shard_map/ppermute | solution.py:215
  292.8 14.6 %collective-permute-start.28 = (bf16[4,96,768]{2,1,0:T(8,128)(2,1)}, bf16[4,96,768]{2,1,0:T(8,128)(2,1)}, u32[]{:S(2)}, u32[]{:S(2)}) collective-permute-start(bf16[4,96,768]{2,1,0:T(8,128)(2,1)} %slice_bitcast_fusion.4), channel_id=1, source_target_pairs={{0,16},{4,20},{8,24},{12,28},{16,0},{20,4},{24,8},{28,12},{1,17},{... | collective-permute-start | bytes 1769480 | tf_op jit(solution)/shard_map/ppermute | solution.py:215
  294.1 15.7 %collective-permute-start.27 = (bf16[4,96,768]{2,1,0:T(8,128)(2,1)}, bf16[4,96,768]{2,1,0:T(8,128)(2,1)}, u32[]{:S(2)}, u32[]{:S(2)}) collective-permute-start(bf16[4,96,768]{2,1,0:T(8,128)(2,1)} %slice_bitcast_fusion.5), channel_id=1, source_target_pairs={{0,8},{4,12},{8,0},{12,4},{16,24},{20,28},{24,16},{28,20},{1,9},{5... | collective-permute-start | bytes 1769480 | tf_op jit(solution)/shard_map/ppermute | solution.py:215
  312.1 22.7 %collective-permute-start.36 = (bf16[216,768]{1,0:T(8,128)(2,1)}, bf16[216,768]{1,0:T(8,128)(2,1)}, u32[]{:S(2)}, u32[]{:S(2)}) collective-permute-start(bf16[216,768]{1,0:T(8,128)(2,1)} %maximum_maximum_fusion.1), channel_id=1, source_target_pairs={{0,3},{1,0},{2,1},{3,2},{4,7},{5,4},{6,5},{7,6},{8,11},{9,8},{10,9... | collective-permute-start | bytes 995336 | tf_op jit(solution)/shard_map/ppermute | solution.py:225
  315.6 62.2 %collective-permute-start.37 = (bf16[216,768]{1,0:T(8,128)(2,1)}, bf16[216,768]{1,0:T(8,128)(2,1)}, u32[]{:S(2)}, u32[]{:S(2)}) collective-permute-start(bf16[216,768]{1,0:T(8,128)(2,1)} %maximum_maximum_fusion.2), channel_id=1, source_target_pairs={{0,2},{1,3},{2,0},{3,1},{4,6},{5,7},{6,4},{7,5},{8,10},{9,11},{10,... | collective-permute-start | bytes 995336 | tf_op jit(solution)/shard_map/ppermute | solution.py:225
  324.2 53.7 %collective-permute-start.38 = (bf16[216,768]{1,0:T(8,128)(2,1)}, bf16[216,768]{1,0:T(8,128)(2,1)}, u32[]{:S(2)}, u32[]{:S(2)}) collective-permute-start(bf16[216,768]{1,0:T(8,128)(2,1)} %maximum_maximum_fusion.3), channel_id=1, source_target_pairs={{0,1},{1,2},{2,3},{3,0},{4,5},{5,6},{6,7},{7,4},{8,9},{9,10},{10,1... | collective-permute-start | bytes 995336 | tf_op jit(solution)/shard_map/ppermute | solution.py:225
  329.9 50.8 %collective-permute-start.30 = (bf16[1,2,2,96,576]{4,3,2,1,0:T(8,128)(2,1)S(1)}, bf16[1,2,2,96,576]{4,3,2,1,0:T(8,128)(2,1)S(1)}, u32[]{:S(2)}, u32[]{:S(2)}) collective-permute-start(bf16[1,2,2,96,576]{4,3,2,1,0:T(8,128)(2,1)S(1)} %slice_bitcast_fusion.6), channel_id=1, source_target_pairs={{0,4},{4,0},{8,12},{12,8},{16,20},{20,16},{24,28},{28,24},{1,5},{5... | collective-permute-start | bytes 1327112 | tf_op jit(solution)/shard_map/ppermute | solution.py:215
  (102 other events, 777.4 us)
Sparse Core Ops, SparseCore 0:
  12.5 87.8 all-gather.1
  296.3 83.3 reduce-scatter.1

commit v3 on v2

--- a/solution.py
+++ b/solution.py
@@ -483,10 +483,6 @@
         for d in range(tensor_size)
     ]
     pieces = exchange(pieces)
-    d_shard = sum(came.astype(F32) for came in pieces)
-    d_fc = d_shard[:owned]
-    d_proj = d_shard[owned : 2 * owned].T
-    d_out = unfold(d_shard[2 * owned :], head_width).T
 
     sums = jnp.sum(stacked, axis=0, dtype=F32)
     sums_by = sums.reshape(local_heads, 3, HEAD_DIM).transpose(1, 0, 2).reshape(3, head_width)
@@ -524,8 +520,14 @@
         jnp.concatenate([rows, placed_fc.reshape(-1), sum_qv.reshape(-1)]), "dp"
     )
     sum_qv = sums_all[rows.size + placed_fc.size :].reshape(2, head_width)
-    sums_all = after(sums_all[: rows.size + placed_fc.size], pieces)
+    sums_all, pieces[1::2], d_qkv = lax.optimization_barrier(
+        (sums_all[: rows.size + placed_fc.size], pieces[1::2], d_qkv)
+    )
     sums_all = total(sums_all, "tensor")
+    d_shard = sum(came.astype(F32) for came in pieces)
+    d_fc = d_shard[:owned]
+    d_proj = d_shard[owned : 2 * owned].T
+    d_out = unfold(d_shard[2 * owned :], head_width).T
     d_gain_two, d_shift_two, d_b_out, d_b_proj, d_gain_one, d_shift_one = (
         sums_all[: 6 * wide].reshape(6, wide)
     )

time: 411 us -> 405 us (0.985)
  waiting for transfers between devices: 138 us -> 115 us
  starting transfers between devices: 51.1 us -> 64.4 us
  local copies, waits for them, and re-layouts: 42.7 us -> 48.4 us
    ppermute x12, waiting for transfers between devices: 96 us -> 81.8 us  [exchange(): lax.ppermute(blocks[d], 'tensor', [(i, (i + d) % size) for i in range(siz...]
    ppermute x29, starting transfers between devices: 25.6 us -> 36.8 us  [flip(): return lax.ppermute(value, axis, [(i, i ^ 1 << bit) for i in range(size)])]
    ppermute x29, waiting for transfers between devices: 42 us -> 32.8 us  [flip(): return lax.ppermute(value, axis, [(i, i ^ 1 << bit) for i in range(size)])]
    unnamed x190 -> x200, local copies, waits for them, and re-layouts: 8.92 us -> 8.82 us
  transfers between devices with their start and end apart: 43 -> 43, of which waited for: 19 -> 17; matrix products, arithmetic and copies ran while one was open for 26% -> 27% of each run, Pallas kernels for 10% -> 10%
where the time goes in v3:
time: 405 us; the launch traced here: 399 us
  waiting for transfers between devices  115 us (28%)
  starting transfers between devices  64.4 us (16%)
  matrix products  62.7 us (15%)
  other arithmetic  52.5 us (13%)
  local copies, waits for them, and re-layouts  48.4 us (12%)
  Pallas kernels  40.7 us (10%)
  between operations  15.8 us (4%)
    ppermute x12, waiting for transfers between devices, exchange(): lax.ppermute(blocks[d], 'tensor', [(i, (i + d) % size) for i in range(siz...  81.8 us
    pallas_call x4, Pallas kernels, kernel_call(): pl.pallas_call(kernel, out_shape=out_shape, in_specs=[pl.BlockSpec(memory...  40.7 us
    ppermute x29, starting transfers between devices, flip(): return lax.ppermute(value, axis, [(i, i ^ 1 << bit) for i in range(size)])  36.8 us
    ppermute x29, waiting for transfers between devices, flip(): return lax.ppermute(value, axis, [(i, i ^ 1 << bit) for i in range(size)])  32.8 us
    ppermute x12, starting transfers between devices, exchange(): lax.ppermute(blocks[d], 'tensor', [(i, (i + d) % size) for i in range(siz...  27.5 us
    another operation x15, other arithmetic, step(): self.block = jnp.stack([self.block, came], axis=at)  23.1 us
    convert_element_type x11, other arithmetic, step(): self.block = (keep.astype(F32) + came.astype(F32)).astype(BF)  13.5 us
    dot_general x3, matrix products, absolute(): jnp.einsum('td,cd->tc', rows, place.astype(rows.dtype), precision=lax.Pre...  9.33 us
  transfers between devices with their start and end apart: 43, of which 17 were waited for; matrix products, arithmetic and copies ran while one was open for 27% of the time, Pallas kernels for 10%

profile of v3, /device:TPU:0, one launch (start us, length us, event | category | flops | bytes accessed | tf_op | source)
XLA Modules:
  0.0 399.2 jit_solution(17836619914961531439)
XLA Ops:
  12.6 3.0 collective-permute-start.3
  16.8 3.7 collective-permute-start
  23.4 6.0 %collective-permute-done.4 = bf16[1,2,96,576]{2,3,1,0:T(8,128)(2,1)S(1)} collective-permute-done((bf16[1,2,96,576]{2,3,1,0:T(8,128)(2,1)S(1)}, bf16[1,2,96,576]{2,3,1,0:T(8,128)(2,1)S(1)}, u32[]{:S(2)}, u32[]{:S(2)}) %collective-permute-start.4) | collective-permute-done | bytes 221216 | tf_op jit(solution)/shard_map/ppermute | solution.py:215
  34.4 41.0 %collective-permute-done.1 = bf16[217,768]{1,0:T(8,128)(2,1)} collective-permute-done((bf16[217,768]{1,0:T(8,128)(2,1)S(1)}, bf16[217,768]{1,0:T(8,128)(2,1)}, u32[]{:S(2)}, u32[]{:S(2)}) %collective-permute-start.1) | collective-permute-done | bytes 333344 | tf_op jit(solution)/shard_map/ppermute | solution.py:225
  89.4 7.4 %collective-permute-done.6 = bf16[4,96,768]{2,1,0:T(8,128)(2,1)} collective-permute-done((bf16[4,96,768]{2,1,0:T(8,128)(2,1)}, bf16[4,96,768]{2,1,0:T(8,128)(2,1)}, u32[]{:S(2)}, u32[]{:S(2)}) %collective-permute-start.6) | collective-permute-done | bytes 589856 | tf_op jit(solution)/shard_map/ppermute | solution.py:215
  103.2 4.6 %add_convert_fusion.qkv_ref = bf16[2048,576]{1,0:T(8,128)(2,1)S(1)} fusion(bf16[2048,768]{0,1:T(8,128)(2,1)} %all-gather.2.cloned.1.call-done, bf16[768,576]{1,0:T(8,128)(2,1)S(1)} %bitcast.324, f32[576]{0:T(1024)S(1)} %reshape.394), kind=kOutput, calls=%fused_computation.13 | convolution fusion | flops 1814298624 | bytes 6392064 | tf_op jit(solution)/shard_map/dot_general | solution.py:376
  107.8 19.1 %shard_map.254 = (bf16[4,512,192]{2,1,0:T(8,128)(2,1)S(1)}, f32[8,2048]{1,0:T(8,128)S(1)}) custom-call(s32[1]{0:T(128)} %bitcast.2.place_ref, bf16[2048,576]{1,0:T(8,128)(2,1)S(1)} %add_convert_fusion.qkv_ref, s32[1,2048]{1,0:T(1,128)S(1)} %compare_select_fusion.first_ref), custom_call_target="tpu_custom_call" | custom-call | flops 6442450944 | bytes 2363392 | tf_op jit(solution)/shard_map/pallas_call | solution.py:151
  128.5 12.3 %collective-permute-start.13 = (bf16[512,192]{1,0:T(8,128)(2,1)S(1)}, bf16[512,192]{1,0:T(8,128)(2,1)S(1)}, u32[]{:S(2)}, u32[]{:S(2)}) collective-permute-start(bf16[512,192]{1,0:T(8,128)(2,1)S(1)} %get-tuple-element.190), channel_id=1, source_target_pairs={{0,2},{1,3},{2,0},{3,1},{4,6},{5,7},{6,4},{7,5},{8,10},{9,11},{10,... | collective-permute-start | bytes 589832 | tf_op jit(solution)/shard_map/ppermute | solution.py:225
  142.9 2.9 pad_maximum_fusion.4
  146.9 3.3 pad_maximum_fusion.3
  150.2 7.9 %collective-permute-done.13 = bf16[512,192]{1,0:T(8,128)(2,1)S(1)} collective-permute-done((bf16[512,192]{1,0:T(8,128)(2,1)S(1)}, bf16[512,192]{1,0:T(8,128)(2,1)S(1)}, u32[]{:S(2)}, u32[]{:S(2)}) %collective-permute-start.13) | collective-permute-done | bytes 196640 | tf_op jit(solution)/shard_map/ppermute | solution.py:225
  161.2 3.1 copy.156
  177.9 4.5 %pad_maximum_fusion = bf16[4,2,2,2,96,768]{5,4,0,3,2,1:T(8,128)(2,1)S(1)} fusion(bf16[4,1,2,2,96,768]{5,4,0,3,2,1:T(8,128)(2,1)} %bitcast.51, bf16[4,1,2,2,96,768]{5,4,0,3,2,1:T(8,128)(2,1)} %bitcast.50), kind=kLoop, calls=%fused_computation.14 | loop fusion | flops 2359296 | bytes 9437184 | tf_op jit(solution)/shard_map/stack | solution.py:259
  183.2 4.6 %multiply_convert_fusion = (bf16[4,512,768]{2,1,0:T(8,128)(2,1)S(1)}, f32[4,768,512]{1,2,0:T(8,128)S(1)}) fusion(f32[4,768]{1,0:T(4,128)S(1)} %maximum_convert_fusion, bf16[4,768,768]{2,1,0:T(8,128)(2,1)S(1)} %bitcast.321, f32[512,768]{0,1:T(8,128)S(1)} %get-tuple-element.272, f32[768]{0:T(1024)S(1)} %copy-done.69, f32[768]{0:T(1024)S(1)} %copy-done.50, ...), kind=kOutput, calls=%fused_computation.11 | convolution fusion | flops 2433613824 | bytes 15751168 | tf_op jit(solution)/shard_map/td,zdf->ztf/dot_general | solution.py:400
  187.8 6.6 %convert_reduce_fusion = (f32[4,768]{1,0:T(4,128)S(1)}, bf16[4,512,768]{2,1,0:T(8,128)(2,1)S(1)}) fusion(f32[4,768,512]{1,2,0:T(8,128)S(1)} %get-tuple-element.274, f32[4,768]{1,0:T(4,128)S(1)} %maximum_convert_fusion, bf16[4,768,768]{2,1,0:T(8,128)(2,1)S(1)} %bitcast.311, f32[768,512]{1,0:T(8,128)S(1)} %copy-done.17), kind=kOutput, calls=%fused_computation.10 | convolution fusion | flops 2450912256 | bytes 15753216 | tf_op jit(solution)/shard_map/td,zdf->ztf/dot_general | solution.py:409
  194.4 3.8 fusion.89
  198.1 4.9 %convolution_convert_fusion.2 = bf16[4,768,768]{1,2,0:T(8,128)(2,1)} fusion(bf16[4,512,768]{2,1,0:T(8,128)(2,1)S(1)} %get-tuple-element.280, f32[512,768]{0,1:T(8,128)S(1)} %get-tuple-element.272, f32[768]{0:T(1024)S(1)} %copy-done.69, f32[768]{0:T(1024)S(1)} %copy-done.50, f32[512]{0:T(512)S(1)} %add_rsqrt_fusion.1, f32[512]{0:T(512)S(1)} %broadcast_multiply_fusion.5), kind=kOutput, calls=%fused_computation.22 | convolution fusion | flops 2420244480 | bytes 9447424 | tf_op jit(solution)/shard_map/td,ztf->zdf/dot_general | solution.py:421
  203.0 4.3 %convolution_convert_fusion.1 = bf16[4,768,768]{1,2,0:T(8,128)(2,1)} fusion(bf16[4,512,768]{2,1,0:T(8,128)(2,1)S(1)} %get-tuple-element.273, f32[768,512]{1,0:T(8,128)S(1)} %copy-done.17), kind=kOutput, calls=%fused_computation.21 | convolution fusion | flops 2418671616 | bytes 9437184 | tf_op jit(solution)/shard_map/td,ztf->zdf/dot_general | solution.py:421
  207.4 3.0 copy.158
  226.3 3.5 fusion.29
  232.1 6.5 %fusion.13 = f32[512,768]{1,0:T(8,128)} fusion(f32[512,768]{0,1:T(8,128)} %copy-done.25, s32[768]{0:T(1024)S(1)} %copy-done.66), kind=kOutput, calls=%fused_computation.38 | convolution fusion | flops 3624468480 | bytes 3148800 | tf_op jit(solution)/shard_map/td,cd->tc/dot_general | solution.py:336
  238.6 2.9 collective-permute-done.20.refs_3_
  241.5 7.1 %shard_map.255 = bf16[2048,192]{1,0:T(8,128)(2,1)S(1)} custom-call(s32[1]{0:T(128)} %bitcast.2.place_ref, bf16[2048,576]{1,0:T(8,128)(2,1)S(1)} %copy-done.3, bf16[4,512,192]{2,1,0:T(8,128)(2,1)S(1)} %get-tuple-element.65.att_ref, f32[8,2048]{1,0:T(8,128)S(1)} %get-tuple-element.76.lse_ref, s32[1,2048]{1,0:T(1,128)S(1)} %compare_select_fusion.first_ref, ...), custom_call_target="tpu_custom_call" | custom-call | flops 536870912 | bytes 3969024 | tf_op jit(solution)/shard_map/pallas_call | solution.py:151
  252.5 3.3 fusion.8
  260.4 7.1 %shard_map.256 = bf16[2048,192]{1,0:T(8,128)(2,1)S(1)} custom-call(s32[1]{0:T(128)} %bitcast.2.place_ref, bf16[2048,576]{1,0:T(8,128)(2,1)S(1)} %copy-done.3, bf16[4,512,192]{2,1,0:T(8,128)(2,1)S(1)} %get-tuple-element.65.att_ref, f32[8,2048]{1,0:T(8,128)S(1)} %get-tuple-element.76.lse_ref, s32[1,2048]{1,0:T(1,128)S(1)} %compare_select_fusion.first_ref, ...), custom_call_target="tpu_custom_call" | custom-call | flops 536870912 | bytes 3969024 | tf_op jit(solution)/shard_map/pallas_call | solution.py:151
  267.5 7.5 %shard_map.257 = bf16[2048,192]{1,0:T(8,128)(2,1)S(1)} custom-call(s32[1]{0:T(128)} %bitcast.2.place_ref, bf16[2048,576]{1,0:T(8,128)(2,1)S(1)} %copy-done.3, bf16[4,512,192]{2,1,0:T(8,128)(2,1)S(1)} %get-tuple-element.65.att_ref, f32[8,2048]{1,0:T(8,128)S(1)} %get-tuple-element.76.lse_ref, s32[1,2048]{1,0:T(1,128)S(1)} %compare_select_fusion.first_ref, ...), custom_call_target="tpu_custom_call" | custom-call | flops 536870912 | bytes 3969024 | tf_op jit(solution)/shard_map/pallas_call | solution.py:151
  277.6 7.2 %convolution_convert_fusion = bf16[2048,768]{1,0:T(8,128)(2,1)} fusion(bf16[2048,576]{1,0:T(8,128)(2,1)} %pad_maximum_fusion.2, bf16[768,576]{1,0:T(8,128)(2,1)S(1)} %bitcast.326, s32[768]{0:T(1024)S(1)} %copy-done.66), kind=kOutput, calls=%fused_computation.20 | convolution fusion | flops 2494021632 | bytes 6392832 | tf_op jit(solution)/shard_map/te,ce->tc/dot_general | solution.py:465
  298.6 9.0 %collective-permute-done.28 = bf16[4,96,768]{2,1,0:T(8,128)(2,1)} collective-permute-done((bf16[4,96,768]{2,1,0:T(8,128)(2,1)}, bf16[4,96,768]{2,1,0:T(8,128)(2,1)}, u32[]{:S(2)}, u32[]{:S(2)}) %collective-permute-start.28) | collective-permute-done | bytes 589856 | tf_op jit(solution)/shard_map/ppermute | solution.py:215
  315.9 5.8 %fusion.78 = (bf16[768,576]{0,1:T(8,128)(2,1)}, f32[768]{0:T(1024)S(1)}) fusion(f32[768]{0:T(1024)S(1)} %copy-done.55, f32[576]{0:T(1024)S(1)} %convert_reduce_fusion.1, f32[768]{0:T(1024)S(1)} %copy-done.53, bf16[768,576]{0,1:T(8,128)(2,1)S(1)} %copy-done.33, bf16[2048,768]{0,1:T(8,128)(2,1)} %all-gather.2.cloned.1.call-done, ...), kind=kOutput, calls=%fused_computation.227 | convolution fusion | flops 1815035136 | bytes 7286016 | tf_op jit(solution)/shard_map/td,te->de/dot_general | solution.py:490
  340.3 7.2 %collective-permute-done.34 = bf16[216,768]{1,0:T(8,128)(2,1)S(1)} collective-permute-done((bf16[216,768]{1,0:T(8,128)(2,1)S(1)}, bf16[216,768]{1,0:T(8,128)(2,1)S(1)}, u32[]{:S(2)}, u32[]{:S(2)}) %collective-permute-start.34) | collective-permute-done | bytes 331808 | tf_op jit(solution)/shard_map/ppermute | solution.py:225
  347.5 22.7 %collective-permute-done.33 = bf16[216,768]{1,0:T(8,128)(2,1)S(1)} collective-permute-done((bf16[216,768]{1,0:T(8,128)(2,1)S(1)}, bf16[216,768]{1,0:T(8,128)(2,1)S(1)}, u32[]{:S(2)}, u32[]{:S(2)}) %collective-permute-start.33) | collective-permute-done | bytes 331808 | tf_op jit(solution)/shard_map/ppermute | solution.py:225
  370.3 10.0 %collective-permute-start.39 = (f32[7680]{0:T(1024)S(1)}, f32[7680]{0:T(1024)S(1)}, u32[]{:S(2)}, u32[]{:S(2)}) collective-permute-start(f32[7680]{0:T(1024)S(1)} %bitcast.347), channel_id=1, source_target_pairs={{0,1},{1,0},{2,3},{3,2},{4,5},{5,4},{6,7},{7,6},{8,9},{9,8},{10,11... | collective-permute-start | bytes 92168 | tf_op jit(solution)/shard_map/ppermute | solution.py:215
  (430 shorter events, 137.6 us)
Async XLA Ops:
  7.2 96.0 %all-gather.2.cloned.1.call-start = ((), (), s32[]{:S(2)}) async-start(), calls=%async_computation.1 | async-start | bytes 3932160 | tf_op jit(solution)/shard_map/all_gather | solution.py:351
  12.4 376.2 %reduce-scatter.2.cloned.1.call-start = ((), (), s32[]{:S(2)}) async-start(), calls=%async_computation.2 | async-start | bytes 3932160 | tf_op jit(solution)/shard_map/reduce_scatter | solution.py:466
  12.6 9.0 %collective-permute-start.3 = (bf16[1,96,576]{1,2,0:T(8,128)(2,1)S(1)}, bf16[1,96,576]{1,2,0:T(8,128)(2,1)S(1)}, u32[]{:S(2)}, u32[]{:S(2)}) collective-permute-start(bf16[1,96,576]{1,2,0:T(8,128)(2,1)S(1)} %bitcast.338), channel_id=1, source_target_pairs={{0,8},{4,12},{8,0},{12,4},{16,24},{20,28},{24,16},{28,20},{1,9},{5... | collective-permute-start | bytes 331784 | tf_op jit(solution)/shard_map/ppermute | solution.py:215
  16.8 17.6 %collective-permute-start = (bf16[217,768]{1,0:T(8,128)(2,1)S(1)}, bf16[217,768]{1,0:T(8,128)(2,1)S(1)}, u32[]{:S(2)}, u32[]{:S(2)}) collective-permute-start(bf16[217,768]{1,0:T(8,128)(2,1)S(1)} %pad_maximum_fusion.14), channel_id=1, source_target_pairs={{0,3},{1,0},{2,1},{3,2},{4,7},{5,4},{6,5},{7,6},{8,11},{9,8},{10,9... | collective-permute-start | bytes 999944 | tf_op jit(solution)/shard_map/ppermute | solution.py:225
  20.4 55.0 %collective-permute-start.1 = (bf16[217,768]{1,0:T(8,128)(2,1)S(1)}, bf16[217,768]{1,0:T(8,128)(2,1)}, u32[]{:S(2)}, u32[]{:S(2)}) collective-permute-start(bf16[217,768]{1,0:T(8,128)(2,1)S(1)} %pad_maximum_fusion.14), channel_id=1, source_target_pairs={{0,2},{1,3},{2,0},{3,1},{4,6},{5,7},{6,4},{7,5},{8,10},{9,11},{10,... | collective-permute-start | bytes 999944 | tf_op jit(solution)/shard_map/ppermute | solution.py:225
  20.4 55.0 %collective-permute-start.2 = (bf16[217,768]{1,0:T(8,128)(2,1)S(1)}, bf16[217,768]{1,0:T(8,128)(2,1)}, u32[]{:S(2)}, u32[]{:S(2)}) collective-permute-start(bf16[217,768]{1,0:T(8,128)(2,1)S(1)} %pad_maximum_fusion.14), channel_id=1, source_target_pairs={{0,1},{1,2},{2,3},{3,0},{4,5},{5,6},{6,7},{7,4},{8,9},{9,10},{10,1... | collective-permute-start | bytes 999944 | tf_op jit(solution)/shard_map/ppermute | solution.py:225
  77.8 10.2 %collective-permute-start.7 = (bf16[4,96,768]{2,1,0:T(8,128)(2,1)}, bf16[4,96,768]{2,1,0:T(8,128)(2,1)}, u32[]{:S(2)}, u32[]{:S(2)}) collective-permute-start(bf16[4,96,768]{2,1,0:T(8,128)(2,1)} %get-tuple-element.212), channel_id=1, source_target_pairs={{0,16},{4,20},{8,24},{12,28},{16,0},{20,4},{24,8},{28,12},{1,17},{... | collective-permute-start | bytes 1769480 | tf_op jit(solution)/shard_map/ppermute | solution.py:215
  81.8 15.0 %collective-permute-start.6 = (bf16[4,96,768]{2,1,0:T(8,128)(2,1)}, bf16[4,96,768]{2,1,0:T(8,128)(2,1)}, u32[]{:S(2)}, u32[]{:S(2)}) collective-permute-start(bf16[4,96,768]{2,1,0:T(8,128)(2,1)} %get-tuple-element.214), channel_id=1, source_target_pairs={{0,8},{4,12},{8,0},{12,4},{16,24},{20,28},{24,16},{28,20},{1,9},{5... | collective-permute-start | bytes 1769480 | tf_op jit(solution)/shard_map/ppermute | solution.py:215
  99.1 27.8 %collective-permute-start.10 = (bf16[4,2,96,768]{3,2,0,1:T(8,128)(2,1)S(1)}, bf16[4,2,96,768]{3,2,0,1:T(8,128)(2,1)}, u32[]{:S(2)}, u32[]{:S(2)}) collective-permute-start(bf16[4,2,96,768]{3,2,0,1:T(8,128)(2,1)S(1)} %pad_maximum_fusion.7), channel_id=1, source_target_pairs={{0,8},{4,12},{8,0},{12,4},{16,24},{20,28},{24,16},{28,20},{1,9},{5... | collective-permute-start | bytes 3538952 | tf_op jit(solution)/shard_map/ppermute | solution.py:215
  101.2 25.7 %collective-permute-start.9 = (bf16[4,2,96,768]{3,2,0,1:T(8,128)(2,1)}, bf16[4,2,96,768]{3,2,0,1:T(8,128)(2,1)}, u32[]{:S(2)}, u32[]{:S(2)}) collective-permute-start(bf16[4,2,96,768]{3,2,0,1:T(8,128)(2,1)} %pad_maximum_fusion.6), channel_id=1, source_target_pairs={{0,16},{4,20},{8,24},{12,28},{16,0},{20,4},{24,8},{28,12},{1,17},{... | collective-permute-start | bytes 3538952 | tf_op jit(solution)/shard_map/ppermute | solution.py:215
  101.7 25.2 %collective-permute-start.11 = (bf16[1,2,96,768]{3,2,1,0:T(8,128)(2,1)S(1)}, bf16[1,2,96,768]{3,2,1,0:T(8,128)(2,1)}, u32[]{:S(2)}, u32[]{:S(2)}) collective-permute-start(bf16[1,2,96,768]{3,2,1,0:T(8,128)(2,1)S(1)} %pad_maximum_fusion.16), channel_id=1, source_target_pairs={{0,16},{4,20},{8,24},{12,28},{16,0},{20,4},{24,8},{28,12},{1,17},{... | collective-permute-start | bytes 884744 | tf_op jit(solution)/shard_map/ppermute | solution.py:215
  127.7 22.5 %collective-permute-start.12 = (bf16[512,192]{1,0:T(8,128)(2,1)S(1)}, bf16[512,192]{1,0:T(8,128)(2,1)S(1)}, u32[]{:S(2)}, u32[]{:S(2)}) collective-permute-start(bf16[512,192]{1,0:T(8,128)(2,1)S(1)} %get-tuple-element.191), channel_id=1, source_target_pairs={{0,3},{1,0},{2,1},{3,2},{4,7},{5,4},{6,5},{7,6},{8,11},{9,8},{10,9... | collective-permute-start | bytes 589832 | tf_op jit(solution)/shard_map/ppermute | solution.py:225
  128.5 29.6 %collective-permute-start.13 = (bf16[512,192]{1,0:T(8,128)(2,1)S(1)}, bf16[512,192]{1,0:T(8,128)(2,1)S(1)}, u32[]{:S(2)}, u32[]{:S(2)}) collective-permute-start(bf16[512,192]{1,0:T(8,128)(2,1)S(1)} %get-tuple-element.190), channel_id=1, source_target_pairs={{0,2},{1,3},{2,0},{3,1},{4,6},{5,7},{6,4},{7,5},{8,10},{9,11},{10,... | collective-permute-start | bytes 589832 | tf_op jit(solution)/shard_map/ppermute | solution.py:225
  140.9 17.3 %collective-permute-start.14 = (bf16[512,192]{1,0:T(8,128)(2,1)S(1)}, bf16[512,192]{1,0:T(8,128)(2,1)S(1)}, u32[]{:S(2)}, u32[]{:S(2)}) collective-permute-start(bf16[512,192]{1,0:T(8,128)(2,1)S(1)} %get-tuple-element.189), channel_id=1, source_target_pairs={{0,1},{1,2},{2,3},{3,0},{4,5},{5,6},{6,7},{7,4},{8,9},{9,10},{10,1... | collective-permute-start | bytes 589832 | tf_op jit(solution)/shard_map/ppermute | solution.py:225
  158.1 16.6 %collective-permute-start.17 = (bf16[4,2,2,96,768]{4,3,0,1,2:T(8,128)(2,1)}, bf16[4,2,2,96,768]{4,3,0,1,2:T(8,128)(2,1)}, u32[]{:S(2)}, u32[]{:S(2)}) collective-permute-start(bf16[4,2,2,96,768]{4,3,0,1,2:T(8,128)(2,1)} %pad_maximum_fusion.4), channel_id=1, source_target_pairs={{0,4},{4,0},{8,12},{12,8},{16,20},{20,16},{24,28},{28,24},{1,5},{5... | collective-permute-start | bytes 7077896 | tf_op jit(solution)/shard_map/ppermute | solution.py:215
  158.4 19.5 %collective-permute-start.16 = (bf16[4,2,2,96,768]{4,3,0,2,1:T(8,128)(2,1)}, bf16[4,2,2,96,768]{4,3,0,2,1:T(8,128)(2,1)}, u32[]{:S(2)}, u32[]{:S(2)}) collective-permute-start(bf16[4,2,2,96,768]{4,3,0,2,1:T(8,128)(2,1)} %pad_maximum_fusion.3), channel_id=1, source_target_pairs={{0,4},{4,0},{8,12},{12,8},{16,20},{20,16},{24,28},{28,24},{1,5},{5... | collective-permute-start | bytes 7077896 | tf_op jit(solution)/shard_map/ppermute | solution.py:215
  161.0 9.6 %collective-permute-start.15 = (bf16[1,2,2,96,768]{4,3,2,1,0:T(8,128)(2,1)S(1)}, bf16[1,2,2,96,768]{4,3,2,1,0:T(8,128)(2,1)S(1)}, u32[]{:S(2)}, u32[]{:S(2)}) collective-permute-start(bf16[1,2,2,96,768]{4,3,2,1,0:T(8,128)(2,1)S(1)} %pad_maximum_fusion.13), channel_id=1, source_target_pairs={{0,4},{4,0},{8,12},{12,8},{16,20},{20,16},{24,28},{28,24},{1,5},{5... | collective-permute-start | bytes 1769480 | tf_op jit(solution)/shard_map/ppermute | solution.py:215
  216.1 13.9 %collective-permute-start.18 = (bf16[512,192]{1,0:T(8,128)(2,1)}, bf16[512,192]{1,0:T(8,128)(2,1)S(1)}, u32[]{:S(2)}, u32[]{:S(2)}) collective-permute-start(bf16[512,192]{1,0:T(8,128)(2,1)} %get-tuple-element.195), channel_id=1, source_target_pairs={{0,3},{1,0},{2,1},{3,2},{4,7},{5,4},{6,5},{7,6},{8,11},{9,8},{10,9... | collective-permute-start | bytes 589832 | tf_op jit(solution)/shard_map/ppermute | solution.py:225
  216.1 22.5 %collective-permute-start.19 = (bf16[512,192]{1,0:T(8,128)(2,1)}, bf16[512,192]{1,0:T(8,128)(2,1)S(1)}, u32[]{:S(2)}, u32[]{:S(2)}) collective-permute-start(bf16[512,192]{1,0:T(8,128)(2,1)} %get-tuple-element.194), channel_id=1, source_target_pairs={{0,2},{1,3},{2,0},{3,1},{4,6},{5,7},{6,4},{7,5},{8,10},{9,11},{10,... | collective-permute-start | bytes 589832 | tf_op jit(solution)/shard_map/ppermute | solution.py:225
  219.5 30.4 %collective-permute-start.22 = (bf16[4,2,2,96,768]{4,3,0,1,2:T(8,128)(2,1)}, bf16[4,2,2,96,768]{4,3,0,1,2:T(8,128)(2,1)}, u32[]{:S(2)}, u32[]{:S(2)}) collective-permute-start(bf16[4,2,2,96,768]{4,3,0,1,2:T(8,128)(2,1)} %bitcast.306), channel_id=1, source_target_pairs={{0,4},{4,0},{8,12},{12,8},{16,20},{20,16},{24,28},{28,24},{1,5},{5... | collective-permute-start | bytes 7077896 | tf_op jit(solution)/shard_map/ppermute | solution.py:215
  223.3 29.2 %collective-permute-start.21 = (bf16[4,2,2,96,768]{4,3,0,2,1:T(8,128)(2,1)}, bf16[4,2,2,96,768]{4,3,0,2,1:T(8,128)(2,1)}, u32[]{:S(2)}, u32[]{:S(2)}) collective-permute-start(bf16[4,2,2,96,768]{4,3,0,2,1:T(8,128)(2,1)} %bitcast.307), channel_id=1, source_target_pairs={{0,4},{4,0},{8,12},{12,8},{16,20},{20,16},{24,28},{28,24},{1,5},{5... | collective-permute-start | bytes 7077896 | tf_op jit(solution)/shard_map/ppermute | solution.py:215
  225.9 22.7 %collective-permute-start.23 = (bf16[1,2,2,96,768]{4,3,2,1,0:T(8,128)(2,1)}, bf16[1,2,2,96,768]{4,3,2,1,0:T(8,128)(2,1)}, u32[]{:S(2)}, u32[]{:S(2)}) collective-permute-start(bf16[1,2,2,96,768]{4,3,2,1,0:T(8,128)(2,1)} %slice_bitcast_fusion.2), channel_id=1, source_target_pairs={{0,4},{4,0},{8,12},{12,8},{16,20},{20,16},{24,28},{28,24},{1,5},{5... | collective-permute-start | bytes 1769480 | tf_op jit(solution)/shard_map/ppermute | solution.py:215
  230.1 11.4 %collective-permute-start.20 = (bf16[512,192]{1,0:T(8,128)(2,1)}, bf16[512,192]{1,0:T(8,128)(2,1)S(1)}, u32[]{:S(2)}, u32[]{:S(2)}) collective-permute-start(bf16[512,192]{1,0:T(8,128)(2,1)} %get-tuple-element.193), channel_id=1, source_target_pairs={{0,1},{1,2},{2,3},{3,0},{4,5},{5,6},{6,7},{7,4},{8,9},{9,10},{10,1... | collective-permute-start | bytes 589832 | tf_op jit(solution)/shard_map/ppermute | solution.py:225
  256.1 28.6 %collective-permute-start.26 = (bf16[1,2,96,768]{3,2,1,0:T(8,128)(2,1)S(1)}, bf16[1,2,96,768]{3,2,1,0:T(8,128)(2,1)S(1)}, u32[]{:S(2)}, u32[]{:S(2)}) collective-permute-start(bf16[1,2,96,768]{3,2,1,0:T(8,128)(2,1)S(1)} %slice_bitcast_fusion.9), channel_id=1, source_target_pairs={{0,16},{4,20},{8,24},{12,28},{16,0},{20,4},{24,8},{28,12},{1,17},{... | collective-permute-start | bytes 884744 | tf_op jit(solution)/shard_map/ppermute | solution.py:215
  257.8 28.0 %collective-permute-start.25 = (bf16[4,2,96,768]{3,2,0,1:T(8,128)(2,1)}, bf16[4,2,96,768]{3,2,0,1:T(8,128)(2,1)}, u32[]{:S(2)}, u32[]{:S(2)}) collective-permute-start(bf16[4,2,96,768]{3,2,0,1:T(8,128)(2,1)} %slice_bitcast_fusion), channel_id=1, source_target_pairs={{0,8},{4,12},{8,0},{12,4},{16,24},{20,28},{24,16},{28,20},{1,9},{5... | collective-permute-start | bytes 3538952 | tf_op jit(solution)/shard_map/ppermute | solution.py:215
  258.9 31.5 %collective-permute-start.24 = (bf16[4,2,96,768]{3,2,0,1:T(8,128)(2,1)}, bf16[4,2,96,768]{3,2,0,1:T(8,128)(2,1)}, u32[]{:S(2)}, u32[]{:S(2)}) collective-permute-start(bf16[4,2,96,768]{3,2,0,1:T(8,128)(2,1)} %slice_bitcast_fusion.1), channel_id=1, source_target_pairs={{0,16},{4,20},{8,24},{12,28},{16,0},{20,4},{24,8},{28,12},{1,17},{... | collective-permute-start | bytes 3538952 | tf_op jit(solution)/shard_map/ppermute | solution.py:215
  293.0 14.6 %collective-permute-start.28 = (bf16[4,96,768]{2,1,0:T(8,128)(2,1)}, bf16[4,96,768]{2,1,0:T(8,128)(2,1)}, u32[]{:S(2)}, u32[]{:S(2)}) collective-permute-start(bf16[4,96,768]{2,1,0:T(8,128)(2,1)} %slice_bitcast_fusion.4), channel_id=1, source_target_pairs={{0,16},{4,20},{8,24},{12,28},{16,0},{20,4},{24,8},{28,12},{1,17},{... | collective-permute-start | bytes 1769480 | tf_op jit(solution)/shard_map/ppermute | solution.py:215
  294.4 15.6 %collective-permute-start.27 = (bf16[4,96,768]{2,1,0:T(8,128)(2,1)}, bf16[4,96,768]{2,1,0:T(8,128)(2,1)}, u32[]{:S(2)}, u32[]{:S(2)}) collective-permute-start(bf16[4,96,768]{2,1,0:T(8,128)(2,1)} %slice_bitcast_fusion.5), channel_id=1, source_target_pairs={{0,8},{4,12},{8,0},{12,4},{16,24},{20,28},{24,16},{28,20},{1,9},{5... | collective-permute-start | bytes 1769480 | tf_op jit(solution)/shard_map/ppermute | solution.py:215
  313.6 66.7 %collective-permute-start.38 = (bf16[216,768]{1,0:T(8,128)(2,1)}, bf16[216,768]{1,0:T(8,128)(2,1)}, u32[]{:S(2)}, u32[]{:S(2)}) collective-permute-start(bf16[216,768]{1,0:T(8,128)(2,1)} %maximum_maximum_fusion.2), channel_id=1, source_target_pairs={{0,2},{1,3},{2,0},{3,1},{4,6},{5,7},{6,4},{7,5},{8,10},{9,11},{10,... | collective-permute-start | bytes 995336 | tf_op jit(solution)/shard_map/ppermute | solution.py:225
  327.8 19.7 %collective-permute-start.34 = (bf16[216,768]{1,0:T(8,128)(2,1)S(1)}, bf16[216,768]{1,0:T(8,128)(2,1)S(1)}, u32[]{:S(2)}, u32[]{:S(2)}) collective-permute-start(bf16[216,768]{1,0:T(8,128)(2,1)S(1)} %maximum_maximum_fusion.1), channel_id=1, source_target_pairs={{0,1},{1,2},{2,3},{3,0},{4,5},{5,6},{6,7},{7,4},{8,9},{9,10},{10,1... | collective-permute-start | bytes 995336 | tf_op jit(solution)/shard_map/ppermute | solution.py:225
  331.1 39.2 %collective-permute-start.33 = (bf16[216,768]{1,0:T(8,128)(2,1)S(1)}, bf16[216,768]{1,0:T(8,128)(2,1)S(1)}, u32[]{:S(2)}, u32[]{:S(2)}) collective-permute-start(bf16[216,768]{1,0:T(8,128)(2,1)S(1)} %maximum_maximum_fusion), channel_id=1, source_target_pairs={{0,3},{1,0},{2,1},{3,2},{4,7},{5,4},{6,5},{7,6},{8,11},{9,8},{10,9... | collective-permute-start | bytes 995336 | tf_op jit(solution)/shard_map/ppermute | solution.py:225
  370.3 12.1 %collective-permute-start.39 = (f32[7680]{0:T(1024)S(1)}, f32[7680]{0:T(1024)S(1)}, u32[]{:S(2)}, u32[]{:S(2)}) collective-permute-start(f32[7680]{0:T(1024)S(1)} %bitcast.347), channel_id=1, source_target_pairs={{0,1},{1,0},{2,3},{3,2},{4,5},{5,4},{6,7},{7,6},{8,9},{9,8},{10,11... | collective-permute-start | bytes 92168 | tf_op jit(solution)/shard_map/ppermute | solution.py:215
  (107 other events, 873.5 us)
Sparse Core Ops, SparseCore 0:
  12.5 87.8 all-gather.1
  298.3 81.9 reduce-scatter.1
